TPU v7x, 256 devices: a whole 4x4x8 slice. The times are simulated.
256 devices in a mesh: ctx: 128 (over x_lo, z, y, core), head: 2 (over x_hi).
Axes of the slice: x: 4 (x_hi: 2, x_lo: 2; x = x_hi * 2 + x_lo), y: 4, z: 8, core: 2. Of those that a mesh axis runs over, the one named last changes fastest.
Arguments:
- queries: bfloat16 [64, 32768, 128], P(None, ('ctx', 'head')), may hold values from -6 to 6
- keys: bfloat16 [8, 32768, 128], P(None, ('ctx', 'head')), may hold values from -6 to 6
- values: bfloat16 [8, 32768, 128], P(None, ('ctx', 'head')), may hold values from -6 to 6
- delta: bfloat16 [64, 32768], P(None, ('ctx', 'head')), may hold values from -270 to 270
- grad_out: bfloat16 [64, 32768, 128], P(None, ('ctx', 'head')), may hold values from -24 to 24
- lse: bfloat16 [64, 32768], P(None, ('ctx', 'head')), may hold values from 6 to 8
Outputs:
- query_grads: bfloat16 [64, 32768, 128], P(None, ('ctx', 'head'))
- key_grads: bfloat16 [8, 32768, 128], P(None, ('ctx', 'head'))
- value_grads: bfloat16 [8, 32768, 128], P(None, ('ctx', 'head'))
All inputs are finite; a program needn't handle non-finite values.
Results may differ from a plain program's by a relative error of at most 0.005.
Values may be sent and summed in bfloat16 or wider, within the bound.
No kernel may reach another device: no remote copies, remote signals or barrier semaphores. Data moves between devices by JAX's collectives and lax.ppermute only.
A program may use at most 128 MiB of HBM per device.

v0:
```python
import math

import jax
import jax.numpy as jnp
from jax import lax
from jax.sharding import PartitionSpec as P


def from_behind(block, axis, distance):
    devices = range(lax.axis_size(axis))
    route = [(i - distance, i) for i in devices if i - distance in devices]
    return lax.ppermute(block, axis, route)


def tile_grads(queries, delta, grads_out, lse, keys, values, allowed):
    heads, rows, width = queries.shape
    groups = keys.shape[0]
    ratio = heads // groups
    scale = 1.0 / math.sqrt(width)
    q_four = queries.reshape(groups, ratio, rows, width)
    g_four = grads_out.reshape(groups, ratio, rows, width)
    delta_f = delta.astype(jnp.float32).reshape(groups, ratio, rows)
    scores = jnp.einsum("kgrd,kjd->kgrj", q_four, keys, preferred_element_type=jnp.float32) * scale
    probs = jnp.exp(scores - lse.astype(jnp.float32).reshape(groups, ratio, rows)[..., None])
    if allowed is not None:
        probs = jnp.where(allowed, probs, 0.0)
    probs_half = probs.astype(jnp.bfloat16)
    dvalue = jnp.einsum("kgrj,kgrd->kjd", probs_half, g_four, preferred_element_type=jnp.float32)
    dprobs = jnp.einsum("kgrd,kjd->kgrj", g_four, values, preferred_element_type=jnp.float32)
    dscores = (probs * (dprobs - delta_f[..., None])).astype(jnp.bfloat16)
    dquery = jnp.einsum("kgrj,kjd->kgrd", dscores, keys, preferred_element_type=jnp.float32) * scale
    dkey = jnp.einsum("kgrj,kgrd->kjd", dscores, q_four, preferred_element_type=jnp.float32) * scale
    return (dquery.reshape(heads, rows, width), dkey, dvalue)


def local(queries, keys, values, delta, grad_out, lse):
    cycle_size = lax.axis_size("ctx")
    offset = cycle_size // 2
    is_late = lax.axis_index("ctx") >= offset
    q_loc, d_loc, g_loc, l_loc, k_loc, v_loc = (
        lax.all_to_all(queries, "head", split_axis=0, concat_axis=1, tiled=True),
        lax.all_to_all(delta, "head", split_axis=0, concat_axis=1, tiled=True),
        lax.all_to_all(grad_out, "head", split_axis=0, concat_axis=1, tiled=True),
        lax.all_to_all(lse, "head", split_axis=0, concat_axis=1, tiled=True),
        lax.all_to_all(keys, "head", split_axis=0, concat_axis=1, tiled=True),
        lax.all_to_all(values, "head", split_axis=0, concat_axis=1, tiled=True),
    )
    rows = q_loc.shape[1]
    query_pos = jnp.arange(rows, dtype=jnp.int32)
    key_pos = jnp.arange(k_loc.shape[1], dtype=jnp.int32)
    allowed = key_pos[None, :] <= query_pos[:, None]
    dq_near, dk_near, dv_near = tile_grads(q_loc, d_loc, g_loc, l_loc, k_loc, v_loc, allowed)
    k_far, v_far = from_behind((k_loc, v_loc), "ctx", offset)
    half = rows // 2
    sent = from_behind(
        (q_loc[:, half:], d_loc[:, half:], g_loc[:, half:], l_loc[:, half:]), "ctx", -offset
    )

    def late_work():
        return tile_grads(
            q_loc[:, :half], d_loc[:, :half], g_loc[:, :half], l_loc[:, :half], k_far, v_far, None
        )

    def early_work():
        return tile_grads(sent[0], sent[1], sent[2], sent[3], k_loc, v_loc, None)

    dq_part, dk_send, dv_send = lax.cond(is_late, late_work, early_work)
    dq_recv = from_behind(dq_part, "ctx", offset)
    dq_far = jnp.where(is_late, jnp.concatenate([dq_part, dq_recv], 1), 0.0)
    dk_keep = jnp.where(is_late, 0.0, dk_send)
    dv_keep = jnp.where(is_late, 0.0, dv_send)
    dk_recv, dv_recv = from_behind((dk_send, dv_send), "ctx", -offset)
    query_grads = (dq_near + dq_far).astype(jnp.bfloat16)
    dk_total = dk_near + (dk_keep + dk_recv)
    dv_total = dv_near + (dv_keep + dv_recv)
    return (
        lax.all_to_all(query_grads, "head", split_axis=1, concat_axis=0, tiled=True),
        lax.all_to_all(
            dk_total.astype(jnp.bfloat16), "head", split_axis=1, concat_axis=0, tiled=True
        ),
        lax.all_to_all(
            dv_total.astype(jnp.bfloat16), "head", split_axis=1, concat_axis=0, tiled=True
        ),
    )


def solution(mesh):
    return jax.shard_map(
        local,
        mesh=mesh,
        in_specs=(
            P(None, ("ctx", "head"), None),
            P(None, ("ctx", "head"), None),
            P(None, ("ctx", "head"), None),
            P(None, ("ctx", "head")),
            P(None, ("ctx", "head"), None),
            P(None, ("ctx", "head")),
        ),
        out_specs=(
            P(None, ("ctx", "head"), None),
            P(None, ("ctx", "head"), None),
            P(None, ("ctx", "head"), None),
        ),
        check_vma=False,
    )
```

profile of v0, /device:TPU:72, one launch (start us, length us, event | category | flops | bytes accessed | tf_op | source)
XLA Modules:
  0.0 232.9 jit_solution(16742395421239299518)
XLA Ops:
  0.6 9.7 %all_to_all.164 = bf16[2,32,128]{2,1,0:T(8,128)(2,1)S(1)} all-to-all(bf16[2,32,128]{2,1,0:T(8,128)(2,1)} %bitcast.174), channel_id=1, replica_groups=mesh['ctx'=128,'head'=2] {'head'}, dimensions={0} | all-to-all | bytes 32768 | tf_op jit(solution)/shard_map/all_to_all | solution.py:44
  10.3 8.6 %all_to_all.165 = bf16[2,32,128]{2,1,0:T(8,128)(2,1)S(1)} all-to-all(bf16[2,32,128]{2,1,0:T(8,128)(2,1)} %bitcast.175), channel_id=1, replica_groups=mesh['ctx'=128,'head'=2] {'head'}, dimensions={0} | all-to-all | bytes 32768 | tf_op jit(solution)/shard_map/all_to_all | solution.py:42
  18.9 10.1 %all_to_all.166 = bf16[8,128,128]{2,1,0:T(8,128)(2,1)S(1)} all-to-all(bf16[8,128,128]{2,1,0:T(8,128)(2,1)} %param.9), channel_id=1, replica_groups=mesh['ctx'=128,'head'=2] {'head'}, dimensions={0} | all-to-all | bytes 524288 | tf_op jit(solution)/shard_map/all_to_all | solution.py:45
  29.0 10.1 %all_to_all.167 = bf16[8,128,128]{2,1,0:T(8,128)(2,1)S(1)} all-to-all(bf16[8,128,128]{2,1,0:T(8,128)(2,1)} %param.10), channel_id=1, replica_groups=mesh['ctx'=128,'head'=2] {'head'}, dimensions={0} | all-to-all | bytes 524288 | tf_op jit(solution)/shard_map/all_to_all | solution.py:46
  39.1 27.4 %all_to_all.168 = bf16[64,128,128]{2,1,0:T(8,128)(2,1)} all-to-all(bf16[64,128,128]{2,1,0:T(8,128)(2,1)} %param.8), channel_id=1, replica_groups=mesh['ctx'=128,'head'=2] {'head'}, dimensions={0} | all-to-all | bytes 4194304 | tf_op jit(solution)/shard_map/all_to_all | solution.py:41
  66.5 4.8 %all-to-all-start.3 = ((bf16[64,128,128]{2,1,0:T(8,128)(2,1)}), bf16[64,128,128]{2,1,0:T(8,128)(2,1)}, u32[]{:S(2)}, u32[]{:S(2)}) async-start(bf16[64,128,128]{2,1,0:T(8,128)(2,1)} %param.12), calls=%async_computation.3 | async-start | bytes 4194304 | tf_op jit(solution)/shard_map/all_to_all | solution.py:43
  71.4 1.3 collective-permute-start.1
  72.7 1.3 collective-permute-start.3
  74.2 0.6 reshape.75
  74.8 0.7 copy.49
  75.5 6.4 %collective-permute-start.4 = (bf16[4,256,128]{2,1,0:T(8,128)(2,1)S(1)}, bf16[4,256,128]{2,1,0:T(8,128)(2,1)}, u32[]{:S(2)}, u32[]{:S(2)}) collective-permute-start(bf16[4,256,128]{2,1,0:T(8,128)(2,1)S(1)} %bitcast.156), channel_id=1, source_target_pairs={{0,128},{2,130},{4,132},{6,134},{8,136},{10,138},{12,140},{14,142}... | collective-permute-start | bytes 786440 | tf_op jit(solution)/shard_map/ppermute | solution.py:12
  82.0 1.8 copy.45
  83.8 1.1 slice.32
  84.9 1.3 collective-permute-start
  86.2 8.9 %all-to-all-done.3 = bf16[64,128,128]{2,1,0:T(8,128)(2,1)} async-done(((bf16[64,128,128]{2,1,0:T(8,128)(2,1)}), bf16[64,128,128]{2,1,0:T(8,128)(2,1)}, u32[]{:S(2)}, u32[]{:S(2)}) %all-to-all-start.3) | async-done | bytes 2097184 | tf_op jit(solution)/shard_map/all_to_all | solution.py:43
  95.0 1.7 copy.48
  96.8 0.0 copy-start.3
  96.8 0.1 slice.34
  96.9 1.3 collective-permute-start.2
  98.2 0.0 copy-start.5
  98.2 0.0 copy-start.6
  98.2 1.3 fusion.38
  99.5 0.0 copy-start.1
  99.5 0.0 collective-permute-done.4
  99.5 6.9 %collective-permute-start.5 = (bf16[4,256,128]{2,1,0:T(8,128)(2,1)S(1)}, bf16[4,256,128]{2,1,0:T(8,128)(2,1)S(1)}, u32[]{:S(2)}, u32[]{:S(2)}) collective-permute-start(bf16[4,256,128]{2,1,0:T(8,128)(2,1)S(1)} %bitcast.169), channel_id=1, source_target_pairs={{0,128},{2,130},{4,132},{6,134},{8,136},{10,138},{12,140},{14,142}... | collective-permute-start | bytes 786440 | tf_op jit(solution)/shard_map/ppermute | solution.py:12
  106.4 4.5 %multiply_convert_fusion.2 = bf16[4,8,256,256]{3,2,1,0:T(8,128)(2,1)} fusion(f32[4,8,256,256]{3,2,1,0:T(8,128)S(1)} %fusion.38, f32[4,8,256]{2,1,0:T(8,128)S(1)} %copy-done.6, f32[4,8,256]{2,1,0:T(8,128)S(1)} %reshape.74, pred[256,256]{1,0:T(8,128)(4,1)S(1)} %iota_compare_fusion, bf16[4,8,256,128]{3,2,1,0:T(8,128)(2,1)S(1)} %bitcast.151, ...), kind=kOutput, calls=%fused_computation.30 | convolution fusion | flops 549453824 | bytes 15073280 | tf_op jit(solution)/shard_map/kgrd,kjd->kgrj/dot_general | solution.py:29
  110.9 0.0 collective-permute-done.5
  110.9 0.0 collective-permute-done.1
  110.9 0.0 collective-permute-done.3
  110.9 8.2 %collective-permute-done = bf16[32,128,128]{2,1,0:T(8,128)(2,1)S(1)} collective-permute-done((bf16[32,128,128]{2,1,0:T(8,128)(2,1)}, bf16[32,128,128]{2,1,0:T(8,128)(2,1)S(1)}, u32[]{:S(2)}, u32[]{:S(2)}) %collective-permute-start) | collective-permute-done | bytes 1048608 | tf_op jit(solution)/shard_map/ppermute | solution.py:12
  119.1 15.9 %collective-permute-done.2 = bf16[32,128,128]{2,1,0:T(8,128)(2,1)S(1)} collective-permute-done((bf16[32,128,128]{2,1,0:T(8,128)(2,1)S(1)}, bf16[32,128,128]{2,1,0:T(8,128)(2,1)S(1)}, u32[]{:S(2)}, u32[]{:S(2)}) %collective-permute-start.2) | collective-permute-done | bytes 1048608 | tf_op jit(solution)/shard_map/ppermute | solution.py:12
  135.0 10.0 %conditional.1 = (f32[4,256,128]{2,1,0:T(8,128)S(1)}, f32[4,256,128]{2,1,0:T(8,128)S(1)}, f32[4,8,128,128]{3,2,1,0:T(8,128)}, f32[]{:T(128)}) conditional(s32[]{:T(128)} %convert_element_type.67, (bf16[32,128,128]{2,1,0:T(8,128)(2,1)S(1)}, bf16[4,256,128]{2,1,0:T(8,128)(2,1)S(1)}, bf16[32,128]{1,0:T(8,128)(2,1)}, bf16[32,128,128]{2,1,0:T(8,128)(2,1)S(1)}, ...), branch_computations={%region_0.1_spmd, %region_1.2_spmd} | conditional | flops 1350574080 | bytes 31293508 | solution.py:67
  135.0 0.7 fusion.11
  135.7 0.7 bitcast_convert_fusion
  136.4 1.7 multiply_convert_fusion
  138.2 2.0 fusion.9
  140.2 2.1 convolution_bitcast_fusion
  142.3 2.6 %fusion.5 = f32[4,256,128]{2,1,0:T(8,128)S(1)} fusion(bf16[4,8,128,128]{3,2,1,0:T(8,128)(2,1)S(1)} %bitcast.163, f32[4,8,128,256]{3,2,1,0:T(8,128)S(1)} %fusion.11, f32[4,8,128]{2,1,0:T(8,128)S(1)} %get-tuple-element.73), kind=kOutput, calls=%fused_computation.7 | convolution fusion | flops 271581184 | bytes 5783552 | tf_op jit(solution)/shard_map/cond/branch_0_fun/kgrj,kgrd->kjd/dot_general | solution.py:28
  145.0 1.9 broadcast_multiply_fusion
  146.9 2.5 %copy.86 = f32[4,8,128,128]{3,1,0,2:T(8,128)} copy(f32[4,8,128,128]{3,2,1,0:T(8,128)S(1)} %broadcast_multiply_fusion) | data formatting | bytes 4194304 | tf_op jit(solution)/shard_map/cond/branch_0_fun/mul | solution.py:31
  149.4 3.2 %collective-permute-start.6 = (f32[32,128,128]{2,0,1:T(8,128)}, f32[32,128,128]{2,0,1:T(8,128)}, u32[]{:S(2)}, u32[]{:S(2)}) collective-permute-start(f32[32,128,128]{2,0,1:T(8,128)} %bitcast.140), channel_id=1, source_target_pairs={{0,128},{2,130},{4,132},{6,134},{8,136},{10,138},{12,140},{14,142}... | collective-permute-start | bytes 6291464 | tf_op jit(solution)/shard_map/ppermute | solution.py:12
  152.6 5.2 %fusion.32 = f32[4,256,128]{2,1,0:T(8,128)} fusion(bf16[4,8,256,128]{3,2,1,0:T(8,128)(2,1)} %bitcast.153, f32[4,8,256,256]{3,2,1,0:T(8,128)S(1)} %copy-done.2, f32[4,8,256]{2,1,0:T(8,128)S(1)} %reshape.74, pred[256,256]{1,0:T(8,128)(4,1)S(1)} %iota_compare_fusion), kind=kOutput, calls=%fused_computation.40 | convolution fusion | flops 545259520 | bytes 11108352 | tf_op jit(solution)/shard_map/kgrj,kgrd->kjd/dot_general | solution.py:28
  157.9 1.3 collective-permute-start.7
  159.2 0.0 copy-done
  159.2 3.2 %convolution_multiply_fusion = f32[4,8,256,128]{3,2,1,0:T(8,128)} fusion(bf16[4,8,256,256]{3,2,1,0:T(8,128)(2,1)S(1)} %copy-done, bf16[4,256,128,1]{2,1,3,0:T(8,128)(2,1)S(1)} %bitcast.159), kind=kOutput, calls=%fused_computation.38 | convolution fusion | flops 537919488 | bytes 8650752 | tf_op jit(solution)/shard_map/kgrj,kjd->kgrd/dot_general | solution.py:31
  162.4 1.3 collective-permute-start.8
  163.7 1.6 fusion.35
  165.3 8.5 %collective-permute-done.7 = f32[4,256,128]{2,1,0:T(8,128)S(1)} collective-permute-done((f32[4,256,128]{2,1,0:T(8,128)S(1)}, f32[4,256,128]{2,1,0:T(8,128)S(1)}, u32[]{:S(2)}, u32[]{:S(2)}) %collective-permute-start.7) | collective-permute-done | bytes 524320 | tf_op jit(solution)/shard_map/ppermute | solution.py:12
  173.8 0.1 add_convert_fusion.1
  173.9 0.9 copy.57
  174.8 4.9 %all-to-all-start.7 = ((bf16[4,256,128]{2,0,1:T(4,128)(2,1)}), bf16[4,256,128]{2,0,1:T(4,128)(2,1)S(1)}, u32[]{:S(2)}, u32[]{:S(2)}) async-start(bf16[4,256,128]{2,0,1:T(4,128)(2,1)} %copy.57), calls=%async_computation.7 | async-start | bytes 524288 | tf_op jit(solution)/shard_map/all_to_all | solution.py:78
  179.7 0.0 collective-permute-done.8
  179.7 1.3 add_convert_fusion
  180.9 0.9 copy.60
  181.9 15.2 %all-to-all-done.7 = bf16[4,256,128]{2,0,1:T(4,128)(2,1)S(1)} async-done(((bf16[4,256,128]{2,0,1:T(4,128)(2,1)}), bf16[4,256,128]{2,0,1:T(4,128)(2,1)S(1)}, u32[]{:S(2)}, u32[]{:S(2)}) %all-to-all-start.7) | async-done | bytes 262176 | tf_op jit(solution)/shard_map/all_to_all | solution.py:78
  197.0 3.4 %all-to-all-start.8 = ((bf16[4,256,128]{2,0,1:T(4,128)(2,1)}), bf16[4,256,128]{2,0,1:T(4,128)(2,1)S(1)}, u32[]{:S(2)}, u32[]{:S(2)}) async-start(bf16[4,256,128]{2,0,1:T(4,128)(2,1)} %copy.60), calls=%async_computation.8 | async-start | bytes 524288 | tf_op jit(solution)/shard_map/all_to_all | solution.py:81
  200.5 0.0 collective-permute-done.6
  200.5 7.4 %fusion.28 = bf16[32,256,128]{2,0,1:T(8,128)(2,1)} fusion(f32[32,128,128]{2,0,1:T(8,128)} %collective-permute-done.6, f32[32,128,128]{2,0,1:T(8,128)} %bitcast.140, f32[32,256,128]{2,1,0:T(8,128)} %bitcast.145, pred[]{:T(512)S(6)} %ge.3), kind=kLoop, calls=%fused_computation.35 | loop fusion | flops 4194304 | bytes 10485761 | tf_op jit(solution)/shard_map/convert_element_type | solution.py:73
  208.0 0.0 all-to-all-done.8
  208.0 4.8 %all-to-all-start.6 = ((bf16[32,256,128]{2,0,1:T(8,128)(2,1)}), bf16[32,256,128]{2,0,1:T(8,128)(2,1)S(1)}, u32[]{:S(2)}, u32[]{:S(2)}) async-start(bf16[32,256,128]{2,0,1:T(8,128)(2,1)} %fusion.28), calls=%async_computation.6 | async-start | bytes 4194304 | tf_op jit(solution)/shard_map/all_to_all | solution.py:77
  212.7 0.7 copy.58
  213.5 0.7 copy.61
  214.2 16.6 %all-to-all-done.6 = bf16[32,256,128]{2,0,1:T(8,128)(2,1)S(1)} async-done(((bf16[32,256,128]{2,0,1:T(8,128)(2,1)}), bf16[32,256,128]{2,0,1:T(8,128)(2,1)S(1)}, u32[]{:S(2)}, u32[]{:S(2)}) %all-to-all-start.6) | async-done | bytes 2097184 | tf_op jit(solution)/shard_map/all_to_all | solution.py:77
  230.8 2.1 copy.55
  (21 shorter events, 0.2 us)
Async XLA Ops:
  66.5 28.6 %all-to-all-start.3 = ((bf16[64,128,128]{2,1,0:T(8,128)(2,1)}), bf16[64,128,128]{2,1,0:T(8,128)(2,1)}, u32[]{:S(2)}, u32[]{:S(2)}) async-start(bf16[64,128,128]{2,1,0:T(8,128)(2,1)} %param.12), calls=%async_computation.3 | async-start | bytes 4194304 | tf_op jit(solution)/shard_map/all_to_all | solution.py:43
  71.4 39.5 %collective-permute-start.1 = (bf16[32,128]{1,0:T(8,128)(2,1)S(1)}, bf16[32,128]{1,0:T(8,128)(2,1)}, u32[]{:S(2)}, u32[]{:S(2)}) collective-permute-start(bf16[32,128]{1,0:T(8,128)(2,1)S(1)} %slice.33), channel_id=1, source_target_pairs={{128,0},{130,2},{132,4},{134,6},{136,8},{138,10},{140,12},{142,14}... | collective-permute-start | bytes 24584 | tf_op jit(solution)/shard_map/ppermute | solution.py:12
  72.7 38.2 %collective-permute-start.3 = (bf16[32,128]{1,0:T(8,128)(2,1)S(1)}, bf16[32,128]{1,0:T(8,128)(2,1)}, u32[]{:S(2)}, u32[]{:S(2)}) collective-permute-start(bf16[32,128]{1,0:T(8,128)(2,1)S(1)} %slice.35), channel_id=1, source_target_pairs={{128,0},{130,2},{132,4},{134,6},{136,8},{138,10},{140,12},{142,14}... | collective-permute-start | bytes 24584 | tf_op jit(solution)/shard_map/ppermute | solution.py:12
  75.5 23.9 %collective-permute-start.4 = (bf16[4,256,128]{2,1,0:T(8,128)(2,1)S(1)}, bf16[4,256,128]{2,1,0:T(8,128)(2,1)}, u32[]{:S(2)}, u32[]{:S(2)}) collective-permute-start(bf16[4,256,128]{2,1,0:T(8,128)(2,1)S(1)} %bitcast.156), channel_id=1, source_target_pairs={{0,128},{2,130},{4,132},{6,134},{8,136},{10,138},{12,140},{14,142}... | collective-permute-start | bytes 786440 | tf_op jit(solution)/shard_map/ppermute | solution.py:12
  84.9 34.3 %collective-permute-start = (bf16[32,128,128]{2,1,0:T(8,128)(2,1)}, bf16[32,128,128]{2,1,0:T(8,128)(2,1)S(1)}, u32[]{:S(2)}, u32[]{:S(2)}) collective-permute-start(bf16[32,128,128]{2,1,0:T(8,128)(2,1)} %slice.32), channel_id=1, source_target_pairs={{128,0},{130,2},{132,4},{134,6},{136,8},{138,10},{140,12},{142,14}... | collective-permute-start | bytes 3145736 | tf_op jit(solution)/shard_map/ppermute | solution.py:12
  96.8 38.2 %copy-start.3 = (bf16[2,32,128,128]{3,2,0,1:T(8,128)(2,1)}, bf16[2,32,128,128]{3,2,0,1:T(8,128)(2,1)S(1)}, u32[]{:S(2)}) copy-start(bf16[2,32,128,128]{3,2,0,1:T(8,128)(2,1)S(1)} %copy.48) | copy-start | bytes 6291460
  96.9 38.1 %collective-permute-start.2 = (bf16[32,128,128]{2,1,0:T(8,128)(2,1)S(1)}, bf16[32,128,128]{2,1,0:T(8,128)(2,1)S(1)}, u32[]{:S(2)}, u32[]{:S(2)}) collective-permute-start(bf16[32,128,128]{2,1,0:T(8,128)(2,1)S(1)} %slice.34), channel_id=1, source_target_pairs={{128,0},{130,2},{132,4},{134,6},{136,8},{138,10},{140,12},{142,14}... | collective-permute-start | bytes 3145736 | tf_op jit(solution)/shard_map/ppermute | solution.py:12
  98.2 1.3 copy-start.5
  98.2 8.2 %copy-start.6 = (f32[4,8,256]{2,1,0:T(8,128)S(1)}, f32[4,8,256]{2,1,0:T(8,128)}, u32[]{:S(2)}) copy-start(f32[4,8,256]{2,1,0:T(8,128)} %reshape.75) | copy-start | bytes 98308
  99.5 11.4 %copy-start.1 = (f32[4,8,256,256]{3,2,1,0:T(8,128)}, f32[4,8,256,256]{3,2,1,0:T(8,128)S(1)}, u32[]{:S(2)}) copy-start(f32[4,8,256,256]{3,2,1,0:T(8,128)S(1)} %fusion.38) | copy-start | bytes 25165828
  99.5 11.4 %collective-permute-start.5 = (bf16[4,256,128]{2,1,0:T(8,128)(2,1)S(1)}, bf16[4,256,128]{2,1,0:T(8,128)(2,1)S(1)}, u32[]{:S(2)}, u32[]{:S(2)}) collective-permute-start(bf16[4,256,128]{2,1,0:T(8,128)(2,1)S(1)} %bitcast.169), channel_id=1, source_target_pairs={{0,128},{2,130},{4,132},{6,134},{8,136},{10,138},{12,140},{14,142}... | collective-permute-start | bytes 786440 | tf_op jit(solution)/shard_map/ppermute | solution.py:12
  135.0 3.2 %copy-start.4 = (bf16[32,128,128]{2,1,0:T(8,128)(2,1)}, bf16[32,128,128]{2,1,0:T(8,128)(2,1)S(1)}, u32[]{:S(2)}) copy-start(bf16[32,128,128]{2,1,0:T(8,128)(2,1)S(1)} %get-tuple-element.49) | copy-start | bytes 3145732 | tf_op jit(solution)/shard_map/cond
  145.0 7.7 %copy-start.2 = (f32[4,8,256,256]{3,2,1,0:T(8,128)S(1)}, f32[4,8,256,256]{3,2,1,0:T(8,128)}, u32[]{:S(2)}) copy-start(f32[4,8,256,256]{3,2,1,0:T(8,128)} %copy-done.1) | copy-start | bytes 25165828
  149.4 9.8 %copy-start = (bf16[4,8,256,256]{3,2,1,0:T(8,128)(2,1)S(1)}, bf16[4,8,256,256]{3,2,1,0:T(8,128)(2,1)}, u32[]{:S(2)}) copy-start(bf16[4,8,256,256]{3,2,1,0:T(8,128)(2,1)} %multiply_convert_fusion.2) | copy-start | bytes 12582916
  149.4 51.1 %collective-permute-start.6 = (f32[32,128,128]{2,0,1:T(8,128)}, f32[32,128,128]{2,0,1:T(8,128)}, u32[]{:S(2)}, u32[]{:S(2)}) collective-permute-start(f32[32,128,128]{2,0,1:T(8,128)} %bitcast.140), channel_id=1, source_target_pairs={{0,128},{2,130},{4,132},{6,134},{8,136},{10,138},{12,140},{14,142}... | collective-permute-start | bytes 6291464 | tf_op jit(solution)/shard_map/ppermute | solution.py:12
  157.9 15.9 %collective-permute-start.7 = (f32[4,256,128]{2,1,0:T(8,128)S(1)}, f32[4,256,128]{2,1,0:T(8,128)S(1)}, u32[]{:S(2)}, u32[]{:S(2)}) collective-permute-start(f32[4,256,128]{2,1,0:T(8,128)S(1)} %broadcast_multiply_fusion.1), channel_id=1, source_target_pairs={{128,0},{130,2},{132,4},{134,6},{136,8},{138,10},{140,12},{142,14}... | collective-permute-start | bytes 1572872 | tf_op jit(solution)/shard_map/ppermute | solution.py:12
  162.4 17.3 %collective-permute-start.8 = (f32[4,256,128]{2,1,0:T(8,128)S(1)}, f32[4,256,128]{2,1,0:T(8,128)}, u32[]{:S(2)}, u32[]{:S(2)}) collective-permute-start(f32[4,256,128]{2,1,0:T(8,128)S(1)} %get-tuple-element.71), channel_id=1, source_target_pairs={{128,0},{130,2},{132,4},{134,6},{136,8},{138,10},{140,12},{142,14}... | collective-permute-start | bytes 1572872 | tf_op jit(solution)/shard_map/ppermute | solution.py:12
  174.8 22.2 %all-to-all-start.7 = ((bf16[4,256,128]{2,0,1:T(4,128)(2,1)}), bf16[4,256,128]{2,0,1:T(4,128)(2,1)S(1)}, u32[]{:S(2)}, u32[]{:S(2)}) async-start(bf16[4,256,128]{2,0,1:T(4,128)(2,1)} %copy.57), calls=%async_computation.7 | async-start | bytes 524288 | tf_op jit(solution)/shard_map/all_to_all | solution.py:78
  197.0 10.9 %all-to-all-start.8 = ((bf16[4,256,128]{2,0,1:T(4,128)(2,1)}), bf16[4,256,128]{2,0,1:T(4,128)(2,1)S(1)}, u32[]{:S(2)}, u32[]{:S(2)}) async-start(bf16[4,256,128]{2,0,1:T(4,128)(2,1)} %copy.60), calls=%async_computation.8 | async-start | bytes 524288 | tf_op jit(solution)/shard_map/all_to_all | solution.py:81
  208.0 22.9 %all-to-all-start.6 = ((bf16[32,256,128]{2,0,1:T(8,128)(2,1)}), bf16[32,256,128]{2,0,1:T(8,128)(2,1)S(1)}, u32[]{:S(2)}, u32[]{:S(2)}) async-start(bf16[32,256,128]{2,0,1:T(8,128)(2,1)} %fusion.28), calls=%async_computation.6 | async-start | bytes 4194304 | tf_op jit(solution)/shard_map/all_to_all | solution.py:77
where the time goes:
time: 234 us; the launch traced here: 233 us
  waiting for transfers between devices  73.3 us (31%)
  blocking collectives  65.9 us (28%)
  starting transfers between devices  42.2 us (18%)
  matrix products  24.9 us (11%)
  local copies, waits for them, and re-layouts  14.2 us (6%)
  other arithmetic  11.5 us (5%)
    ppermute x9, waiting for transfers between devices, from_behind(): return lax.ppermute(block, axis, route)  32.6 us
    all_to_all x1, blocking collectives, local(): lax.all_to_all(queries, 'head', split_axis=0, concat_axis=1, tiled=True)  27.4 us
    ppermute x9, starting transfers between devices, from_behind(): return lax.ppermute(block, axis, route)  24.2 us
    all_to_all x1, waiting for transfers between devices, local(): lax.all_to_all(query_grads, 'head', split_axis=1, concat_axis=0, tiled=True)  16.6 us
    all_to_all x1, waiting for transfers between devices, local(): lax.all_to_all(dk_total.astype(jnp.bfloat16), 'head', split_axis=1, conca...  15.2 us
    all_to_all x1, blocking collectives, local(): lax.all_to_all(values, 'head', split_axis=0, concat_axis=1, tiled=True)  10.1 us
    all_to_all x1, blocking collectives, local(): lax.all_to_all(keys, 'head', split_axis=0, concat_axis=1, tiled=True)  10.1 us
    all_to_all x1, blocking collectives, local(): lax.all_to_all(lse, 'head', split_axis=0, concat_axis=1, tiled=True)  9.66 us
  transfers between devices with their start and end apart: 13, of which 6 were waited for; matrix products, arithmetic and copies ran while one was open for 15% of the time, Pallas kernels for 0%

commit v1 on v0

v1 whole, which is shorter than its diff:
```python
import functools
import math

import jax
import jax.numpy as jnp
from jax import lax
from jax.experimental import pallas as pl
from jax.experimental.pallas import tpu as pltpu
from jax.sharding import PartitionSpec as P

LOG2E = math.log2(math.e)
NN = (((1,), (0,)), ((), ()))
NT = (((1,), (1,)), ((), ()))
TN = (((0,), (0,)), ((), ()))
AXES = ("ctx", "head")


def dot(a, b, dims):
    return lax.dot_general(a, b, dims, preferred_element_type=jnp.float32)


def route(x, pairs):
    far = lax.axis_size("ctx") // 2

    def device(role, c):
        return (c + (far if role[0] == "L" else 0)) * 2 + int(role[1])

    table = []
    for pair in pairs.split():
        src, dst = pair.split(">")
        table += [(device(src, c), device(dst, c)) for c in range(far)]
    return lax.ppermute(x, AXES, table)


def head_tiles(q_ref, g_ref, lse, delta, g, ratio):
    rows = q_ref.shape[1]
    lo = g * ratio
    width = q_ref.shape[2]
    q = q_ref[lo : lo + ratio].reshape(ratio * rows, width)
    g_out = g_ref[lo : lo + ratio].reshape(ratio * rows, width)
    lse_row = jnp.concatenate([lse[lo + i : lo + i + 1, :] for i in range(ratio)], 1)
    delta_row = jnp.concatenate([delta[lo + i : lo + i + 1, :] for i in range(ratio)], 1)
    return q, g_out, lse_row, delta_row


def grads(q, g_out, lse_row, delta_row, k, v, causal, rows):
    scale = 1.0 / math.sqrt(q.shape[1])
    probs = jnp.exp2(dot(k, q, NT) * (scale * LOG2E) - lse_row)
    if causal:
        key = lax.broadcasted_iota(jnp.int32, probs.shape, 0)
        row = lax.broadcasted_iota(jnp.int32, probs.shape, 1) % rows
        probs = jnp.where(key <= row, probs, 0.0)
    dprobs = dot(v, g_out, NT)
    dscores = (probs * (dprobs - delta_row)).astype(jnp.bfloat16)
    dvalue = dot(probs.astype(jnp.bfloat16), g_out, NN)
    dkey = dot(dscores, q, NN) * scale
    dquery = dot(dscores, k, TN) * scale
    return dquery, dkey, dvalue


def unit_kernel(causal, flag_at, ratio, flags, *refs):
    q_ref, g_ref, lse_ref, delta_ref = refs[:4]
    refs = refs[4:]
    dq_in = None
    if flag_at is not None:
        dq_in, refs = refs[0], refs[1:]
    n = (len(refs) - 1) // 2
    kv_refs, dq_ref, out_refs = refs[:n], refs[n], refs[n + 1 :]
    rows, width = q_ref.shape[1:]
    groups = q_ref.shape[0] // ratio

    def work():
        lse = lse_ref[...].astype(jnp.float32) * LOG2E
        delta = delta_ref[...].astype(jnp.float32)
        for g in range(groups):
            q, g_out, lse_row, delta_row = head_tiles(q_ref, g_ref, lse, delta, g, ratio)
            k = jnp.concatenate([r[0, g] for r in kv_refs], 0)
            v = jnp.concatenate([r[1, g] for r in kv_refs], 0)
            dq, dk, dv = grads(q, g_out, lse_row, delta_row, k, v, causal, rows)
            dq = dq.reshape(ratio, rows, width)
            at = slice(g * ratio, (g + 1) * ratio)
            if dq_in is not None:
                dq = dq + dq_in[at]
            dq_ref[at] = dq.astype(dq_ref.dtype)
            for i, out in enumerate(out_refs):
                cut = slice(i * rows, (i + 1) * rows)
                out[0, g] = dk[cut].astype(out.dtype)
                out[1, g] = dv[cut].astype(out.dtype)

    if flag_at is None:
        work()
    else:
        pl.when(flags[flag_at] == 1)(work)

        @pl.when(flags[flag_at] == 0)
        def _():
            dq_ref[...] = dq_in[...].astype(dq_ref.dtype)


def unit_call(name, flags, q, g_out, lse, delta, dq_in, kvs, *, causal, flag_at, dq_dtype, kv_dtype,
              first=0, dq_alias=None, step=2):
    heads, rows, width = q.shape
    groups = kvs[0].shape[1]
    all_groups = 8 * heads // 64
    ratio = heads // all_groups
    off = first // step
    heads_block = pl.BlockSpec((step * ratio, rows, width), lambda i, f: (i + off, 0, 0))
    rows_block = pl.BlockSpec((step * ratio, rows), lambda i, f: (i + off, 0))
    kv_block = pl.BlockSpec((2, step, rows, width), lambda i, f: (0, i, 0, 0))
    args = [q, g_out, lse, delta]
    in_specs = [heads_block, heads_block, rows_block, rows_block]
    if dq_in is not None:
        args.append(dq_in)
        in_specs.append(heads_block)
    args += kvs
    in_specs += [kv_block] * len(kvs)
    aliases = {}
    kernel = functools.partial(unit_kernel, causal, flag_at, ratio)
    if dq_alias is not None:
        aliases = {len(args) + 1: 0}
        args.append(dq_alias)
        in_specs.append(pl.BlockSpec(memory_space=pl.ANY))
        inner, drop = kernel, len(args)

        def kernel(flags, *refs):
            inner(flags, *refs[: drop - 1], *refs[drop:])

    pairs = len(kvs) * groups * ratio * rows * rows
    return pl.pallas_call(
        kernel,
        grid_spec=pltpu.PrefetchScalarGridSpec(
            num_scalar_prefetch=1,
            grid=(groups // step,),
            in_specs=in_specs,
            out_specs=[heads_block] + [kv_block] * len(kvs),
        ),
        out_shape=[jax.ShapeDtypeStruct(q.shape, dq_dtype)]
        + [jax.ShapeDtypeStruct(kvs[0].shape, kv_dtype)] * len(kvs),
        input_output_aliases=aliases,
        compiler_params=pltpu.CompilerParams(vmem_limit_bytes=40 << 20),
        cost_estimate=pl.CostEstimate(
            flops=10 * pairs * width, bytes_accessed=8 << 20, transcendentals=pairs
        ),
        name=name,
    )(flags, *args)


def local(queries, keys, values, delta, grad_out, lse):
    half = lax.axis_index("head")
    is_late = lax.axis_index("ctx") >= lax.axis_size("ctx") // 2
    flags = jnp.stack([half.astype(jnp.int32), is_late.astype(jnp.int32)])
    kv = jnp.stack([keys, values])
    kv_z = route(kv, "E0>E1 L0>L1")
    kv_x = route(kv, "E0>L0 E1>L1")
    kv_y = route(kv, "E0>L1 E1>L0")
    call = functools.partial(unit_call, flags=flags, q=queries, g_out=grad_out, lse=lse, delta=delta)
    dq, dkv = call("diag", dq_in=None, kvs=[kv], causal=True, flag_at=None,
                   dq_dtype=jnp.float32, kv_dtype=jnp.float32)
    dq, dz = call("near", dq_in=dq, kvs=[kv_z], causal=False, flag_at=0,
                  dq_dtype=jnp.float32, kv_dtype=jnp.bfloat16)
    rz = route(dz, "E1>E0 L1>L0")
    dq, dx, dy = call("far", dq_in=dq, kvs=[kv_x, kv_y], causal=False, flag_at=1,
                      dq_dtype=jnp.bfloat16, kv_dtype=jnp.bfloat16)
    rx = route(dx, "L0>E0 L1>E1")
    ry = route(dy, "L1>E0 L0>E1")
    f32 = jnp.float32
    total = dkv + rz.astype(f32) + (rx.astype(f32) + ry.astype(f32))
    total = total.astype(jnp.bfloat16)
    return dq, total[0], total[1]


def solution(mesh):
    spec3 = P(None, AXES, None)
    spec2 = P(None, AXES)
    return jax.shard_map(
        local,
        mesh=mesh,
        in_specs=(spec3, spec3, spec3, spec2, spec3, spec2),
        out_specs=(spec3, spec3, spec3),
        check_vma=False,
    )
```

time: 234 us -> 66.4 us (0.28)
  the two profiles are of different devices: /device:TPU:72 before, /device:TPU:42 now
where the time goes in v1:
time: 66.4 us; the launch traced here: 66.1 us
  waiting for transfers between devices  33.6 us (51%)
  Pallas kernels  14.2 us (21%)
  starting transfers between devices  10.6 us (16%)
  local copies, waits for them, and re-layouts  5.45 us (8%)
  other arithmetic  1.47 us (2%)
  between operations  0.73 us (1%)
    ppermute x6, waiting for transfers between devices, route(): return lax.ppermute(x, AXES, table)  33.6 us
    pallas_call x3, Pallas kernels, unit_call(): pl.pallas_call(kernel, grid_spec=pltpu.PrefetchScalarGridSpec(num_scalar_...  14.2 us
    ppermute x6, starting transfers between devices, route(): return lax.ppermute(x, AXES, table)  10.6 us
    unnamed x8, local copies, waits for them, and re-layouts  4.62 us
  transfers between devices with their start and end apart: 6, of which 4 were waited for; matrix products, arithmetic and copies ran while one was open for 0% of the time, Pallas kernels for 9%

profile of v1, /device:TPU:42, one launch (start us, length us, event | category | flops | bytes accessed | tf_op | source)
XLA Modules:
  0.0 66.1 jit_solution(17717761515991856492)
XLA Ops:
  0.6 1.1 %pad_maximum_fusion.refs_4_ = bf16[2,8,128,128]{3,2,1,0:T(8,128)(2,1)S(1)} fusion(bf16[1,8,128,128]{3,2,1,0:T(8,128)(2,1)} %bitcast.8, bf16[1,8,128,128]{3,2,1,0:T(8,128)(2,1)} %bitcast.9), kind=kLoop, calls=%fused_computation.1 | loop fusion | flops 262144 | bytes 1048576 | tf_op jit(solution)/shard_map/stack | solution.py:152
  1.7 4.1 %collective-permute-start = (bf16[2,8,128,128]{3,2,1,0:T(8,128)(2,1)S(1)}, bf16[2,8,128,128]{3,2,1,0:T(8,128)(2,1)S(1)}, u32[]{:S(2)}, u32[]{:S(2)}) collective-permute-start(bf16[2,8,128,128]{3,2,1,0:T(8,128)(2,1)S(1)} %pad_maximum_fusion.refs_4_), channel_id=1, source_target_pairs={{0,1},{2,3},{4,5},{6,7},{8,9},{10,11},{12,13},{14,15},{16,17},{18,... | collective-permute-start | bytes 1572872 | tf_op jit(solution)/shard_map/ppermute | solution.py:32
  5.8 1.3 %collective-permute-start.1 = (bf16[2,8,128,128]{3,2,1,0:T(8,128)(2,1)S(1)}, bf16[2,8,128,128]{3,2,1,0:T(8,128)(2,1)S(1)}, u32[]{:S(2)}, u32[]{:S(2)}) collective-permute-start(bf16[2,8,128,128]{3,2,1,0:T(8,128)(2,1)S(1)} %pad_maximum_fusion.refs_4_), channel_id=1, source_target_pairs={{0,128},{2,130},{4,132},{6,134},{8,136},{10,138},{12,140},{14,142}... | collective-permute-start | bytes 1572872 | tf_op jit(solution)/shard_map/ppermute | solution.py:32
  7.1 1.3 %collective-permute-start.2 = (bf16[2,8,128,128]{3,2,1,0:T(8,128)(2,1)S(1)}, bf16[2,8,128,128]{3,2,1,0:T(8,128)(2,1)S(1)}, u32[]{:S(2)}, u32[]{:S(2)}) collective-permute-start(bf16[2,8,128,128]{3,2,1,0:T(8,128)(2,1)S(1)} %pad_maximum_fusion.refs_4_), channel_id=1, source_target_pairs={{0,129},{2,131},{4,133},{6,135},{8,137},{10,139},{12,141},{14,143}... | collective-permute-start | bytes 1572872 | tf_op jit(solution)/shard_map/ppermute | solution.py:32
  8.4 0.1 pad_add_fusion.flags
  8.5 0.0 copy-start
  8.5 1.6 %copy-done = bf16[64,128,128]{2,1,0:T(8,128)(2,1)S(1)} copy-done((bf16[64,128,128]{2,1,0:T(8,128)(2,1)S(1)}, bf16[64,128,128]{2,1,0:T(8,128)(2,1)}, u32[]{:S(2)}) %copy-start) | copy-done | bytes 2097176
  10.1 0.0 copy-start.1
  10.1 1.6 %copy-done.1 = bf16[64,128,128]{2,1,0:T(8,128)(2,1)S(1)} copy-done((bf16[64,128,128]{2,1,0:T(8,128)(2,1)S(1)}, bf16[64,128,128]{2,1,0:T(8,128)(2,1)}, u32[]{:S(2)}) %copy-start.1) | copy-done | bytes 2097176
  11.6 0.0 copy-start.2
  11.7 0.7 %copy-done.2 = bf16[64,128]{1,0:T(8,128)(2,1)S(1)} copy-done((bf16[64,128]{1,0:T(8,128)(2,1)S(1)}, bf16[64,128]{1,0:T(8,128)(2,1)}, u32[]{:S(2)}) %copy-start.2) | copy-done | bytes 16408
  12.4 0.0 copy-start.3
  12.4 0.7 %copy-done.3 = bf16[64,128]{1,0:T(8,128)(2,1)S(1)} copy-done((bf16[64,128]{1,0:T(8,128)(2,1)S(1)}, bf16[64,128]{1,0:T(8,128)(2,1)}, u32[]{:S(2)}) %copy-start.3) | copy-done | bytes 16408
  13.1 5.0 %diag.1 = (f32[64,128,128]{2,1,0:T(8,128)S(1)}, f32[2,8,128,128]{3,2,1,0:T(8,128)S(1)}) custom-call(s32[2]{0:T(128)S(1)} %pad_add_fusion.flags, bf16[64,128,128]{2,1,0:T(8,128)(2,1)S(1)} %copy-done, bf16[64,128,128]{2,1,0:T(8,128)(2,1)S(1)} %copy-done.1, bf16[64,128]{1,0:T(8,128)(2,1)S(1)} %copy-done.2, bf16[64,128]{1,0:T(8,128)(2,1)S(1)} %copy-done.3, ...), custom_call_target="tpu_custom_call" | custom-call | flops 1342177280 | bytes 8388608 | tf_op jit(solution)/shard_map/diag/pallas_call | solution.py:129
  18.1 0.0 collective-permute-done.refs_5_
  18.1 1.1 %near.1 = (f32[64,128,128]{2,1,0:T(8,128)S(1)}, bf16[2,8,128,128]{3,2,1,0:T(8,128)(2,1)S(1)}) custom-call(s32[2]{0:T(128)S(1)} %pad_add_fusion.flags, bf16[64,128,128]{2,1,0:T(8,128)(2,1)S(1)} %copy-done, bf16[64,128,128]{2,1,0:T(8,128)(2,1)S(1)} %copy-done.1, bf16[64,128]{1,0:T(8,128)(2,1)S(1)} %copy-done.2, bf16[64,128]{1,0:T(8,128)(2,1)S(1)} %copy-done.3, ...), custom_call_target="tpu_custom_call" | custom-call | flops 1342177280 | bytes 8388608 | tf_op jit(solution)/shard_map/near/pallas_call | solution.py:129
  19.2 10.9 %collective-permute-done.1.refs_5_ = bf16[2,8,128,128]{3,2,1,0:T(8,128)(2,1)S(1)} collective-permute-done((bf16[2,8,128,128]{3,2,1,0:T(8,128)(2,1)S(1)}, bf16[2,8,128,128]{3,2,1,0:T(8,128)(2,1)S(1)}, u32[]{:S(2)}, u32[]{:S(2)}) %collective-permute-start.1) | collective-permute-done | bytes 524320 | tf_op jit(solution)/shard_map/ppermute | solution.py:32
  30.0 0.0 collective-permute-done.2.refs_6_
  30.0 8.2 %far.1 = (bf16[64,128,128]{2,1,0:T(8,128)(2,1)}, bf16[2,8,128,128]{3,2,1,0:T(8,128)(2,1)S(1)}, bf16[2,8,128,128]{3,2,1,0:T(8,128)(2,1)S(1)}) custom-call(s32[2]{0:T(128)S(1)} %pad_add_fusion.flags, bf16[64,128,128]{2,1,0:T(8,128)(2,1)S(1)} %copy-done, bf16[64,128,128]{2,1,0:T(8,128)(2,1)S(1)} %copy-done.1, bf16[64,128]{1,0:T(8,128)(2,1)S(1)} %copy-done.2, ...), custom_call_target="tpu_custom_call" | custom-call | flops 2684354560 | bytes 8388608 | tf_op jit(solution)/shard_map/far/pallas_call | solution.py:129
  38.2 1.3 %collective-permute-start.4 = (bf16[2,8,128,128]{3,2,1,0:T(8,128)(2,1)S(1)}, bf16[2,8,128,128]{3,2,1,0:T(8,128)(2,1)S(1)}, u32[]{:S(2)}, u32[]{:S(2)}) collective-permute-start(bf16[2,8,128,128]{3,2,1,0:T(8,128)(2,1)S(1)} %get-tuple-element.15), channel_id=1, source_target_pairs={{128,0},{130,2},{132,4},{134,6},{136,8},{138,10},{140,12},{142,14}... | collective-permute-start | bytes 1572872 | tf_op jit(solution)/shard_map/ppermute | solution.py:32
  39.5 1.3 %collective-permute-start.5 = (bf16[2,8,128,128]{3,2,1,0:T(8,128)(2,1)S(1)}, bf16[2,8,128,128]{3,2,1,0:T(8,128)(2,1)S(1)}, u32[]{:S(2)}, u32[]{:S(2)}) collective-permute-start(bf16[2,8,128,128]{3,2,1,0:T(8,128)(2,1)S(1)} %get-tuple-element.16), channel_id=1, source_target_pairs={{129,0},{131,2},{133,4},{135,6},{137,8},{139,10},{141,12},{143,14}... | collective-permute-start | bytes 1572872 | tf_op jit(solution)/shard_map/ppermute | solution.py:32
  40.9 1.3 %collective-permute-start.3 = (bf16[2,8,128,128]{3,2,1,0:T(8,128)(2,1)S(1)}, bf16[2,8,128,128]{3,2,1,0:T(8,128)(2,1)S(1)}, u32[]{:S(2)}, u32[]{:S(2)}) collective-permute-start(bf16[2,8,128,128]{3,2,1,0:T(8,128)(2,1)S(1)} %get-tuple-element.14), channel_id=1, source_target_pairs={{1,0},{3,2},{5,4},{7,6},{9,8},{11,10},{13,12},{15,14},{17,16},{19,... | collective-permute-start | bytes 1572872 | tf_op jit(solution)/shard_map/ppermute | solution.py:32
  42.2 7.9 %collective-permute-done.4 = bf16[2,8,128,128]{3,2,1,0:T(8,128)(2,1)S(1)} collective-permute-done((bf16[2,8,128,128]{3,2,1,0:T(8,128)(2,1)S(1)}, bf16[2,8,128,128]{3,2,1,0:T(8,128)(2,1)S(1)}, u32[]{:S(2)}, u32[]{:S(2)}) %collective-permute-start.4) | collective-permute-done | bytes 524320 | tf_op jit(solution)/shard_map/ppermute | solution.py:32
  50.1 1.3 %collective-permute-done.5 = bf16[2,8,128,128]{3,2,1,0:T(8,128)(2,1)S(1)} collective-permute-done((bf16[2,8,128,128]{3,2,1,0:T(8,128)(2,1)S(1)}, bf16[2,8,128,128]{3,2,1,0:T(8,128)(2,1)S(1)}, u32[]{:S(2)}, u32[]{:S(2)}) %collective-permute-start.5) | collective-permute-done | bytes 524320 | tf_op jit(solution)/shard_map/ppermute | solution.py:32
  51.4 13.5 %collective-permute-done.3 = bf16[2,8,128,128]{3,2,1,0:T(8,128)(2,1)S(1)} collective-permute-done((bf16[2,8,128,128]{3,2,1,0:T(8,128)(2,1)S(1)}, bf16[2,8,128,128]{3,2,1,0:T(8,128)(2,1)S(1)}, u32[]{:S(2)}, u32[]{:S(2)}) %collective-permute-start.3) | collective-permute-done | bytes 524320 | tf_op jit(solution)/shard_map/ppermute | solution.py:32
  64.9 0.3 add_convert_fusion
  65.2 0.8 %slice_bitcast_fusion = (bf16[8,128,128]{2,1,0:T(8,128)(2,1)}, bf16[8,128,128]{2,1,0:T(8,128)(2,1)}) fusion(bf16[2,8,128,128]{3,2,1,0:T(8,128)(2,1)S(1)} %add_convert_fusion), kind=kLoop, calls=%fused_computation.2 | loop fusion | bytes 1048576 | tf_op jit(solution)/shard_map/squeeze | solution.py:169
Async XLA Ops:
  1.7 16.4 %collective-permute-start = (bf16[2,8,128,128]{3,2,1,0:T(8,128)(2,1)S(1)}, bf16[2,8,128,128]{3,2,1,0:T(8,128)(2,1)S(1)}, u32[]{:S(2)}, u32[]{:S(2)}) collective-permute-start(bf16[2,8,128,128]{3,2,1,0:T(8,128)(2,1)S(1)} %pad_maximum_fusion.refs_4_), channel_id=1, source_target_pairs={{0,1},{2,3},{4,5},{6,7},{8,9},{10,11},{12,13},{14,15},{16,17},{18,... | collective-permute-start | bytes 1572872 | tf_op jit(solution)/shard_map/ppermute | solution.py:32
  5.8 24.3 %collective-permute-start.1 = (bf16[2,8,128,128]{3,2,1,0:T(8,128)(2,1)S(1)}, bf16[2,8,128,128]{3,2,1,0:T(8,128)(2,1)S(1)}, u32[]{:S(2)}, u32[]{:S(2)}) collective-permute-start(bf16[2,8,128,128]{3,2,1,0:T(8,128)(2,1)S(1)} %pad_maximum_fusion.refs_4_), channel_id=1, source_target_pairs={{0,128},{2,130},{4,132},{6,134},{8,136},{10,138},{12,140},{14,142}... | collective-permute-start | bytes 1572872 | tf_op jit(solution)/shard_map/ppermute | solution.py:32
  7.1 23.0 %collective-permute-start.2 = (bf16[2,8,128,128]{3,2,1,0:T(8,128)(2,1)S(1)}, bf16[2,8,128,128]{3,2,1,0:T(8,128)(2,1)S(1)}, u32[]{:S(2)}, u32[]{:S(2)}) collective-permute-start(bf16[2,8,128,128]{3,2,1,0:T(8,128)(2,1)S(1)} %pad_maximum_fusion.refs_4_), channel_id=1, source_target_pairs={{0,129},{2,131},{4,133},{6,135},{8,137},{10,139},{12,141},{14,143}... | collective-permute-start | bytes 1572872 | tf_op jit(solution)/shard_map/ppermute | solution.py:32
  8.5 1.6 %copy-start = (bf16[64,128,128]{2,1,0:T(8,128)(2,1)S(1)}, bf16[64,128,128]{2,1,0:T(8,128)(2,1)}, u32[]{:S(2)}) copy-start(bf16[64,128,128]{2,1,0:T(8,128)(2,1)} %refs_0_.5) | copy-start | bytes 6291460
  10.1 1.6 %copy-start.1 = (bf16[64,128,128]{2,1,0:T(8,128)(2,1)S(1)}, bf16[64,128,128]{2,1,0:T(8,128)(2,1)}, u32[]{:S(2)}) copy-start(bf16[64,128,128]{2,1,0:T(8,128)(2,1)} %refs_1_.5) | copy-start | bytes 6291460
  11.6 0.7 %copy-start.2 = (bf16[64,128]{1,0:T(8,128)(2,1)S(1)}, bf16[64,128]{1,0:T(8,128)(2,1)}, u32[]{:S(2)}) copy-start(bf16[64,128]{1,0:T(8,128)(2,1)} %refs_2_.5) | copy-start | bytes 49156
  12.4 0.7 %copy-start.3 = (bf16[64,128]{1,0:T(8,128)(2,1)S(1)}, bf16[64,128]{1,0:T(8,128)(2,1)}, u32[]{:S(2)}) copy-start(bf16[64,128]{1,0:T(8,128)(2,1)} %refs_3_.5) | copy-start | bytes 49156
  38.2 11.9 %collective-permute-start.4 = (bf16[2,8,128,128]{3,2,1,0:T(8,128)(2,1)S(1)}, bf16[2,8,128,128]{3,2,1,0:T(8,128)(2,1)S(1)}, u32[]{:S(2)}, u32[]{:S(2)}) collective-permute-start(bf16[2,8,128,128]{3,2,1,0:T(8,128)(2,1)S(1)} %get-tuple-element.15), channel_id=1, source_target_pairs={{128,0},{130,2},{132,4},{134,6},{136,8},{138,10},{140,12},{142,14}... | collective-permute-start | bytes 1572872 | tf_op jit(solution)/shard_map/ppermute | solution.py:32
  39.5 11.9 %collective-permute-start.5 = (bf16[2,8,128,128]{3,2,1,0:T(8,128)(2,1)S(1)}, bf16[2,8,128,128]{3,2,1,0:T(8,128)(2,1)S(1)}, u32[]{:S(2)}, u32[]{:S(2)}) collective-permute-start(bf16[2,8,128,128]{3,2,1,0:T(8,128)(2,1)S(1)} %get-tuple-element.16), channel_id=1, source_target_pairs={{129,0},{131,2},{133,4},{135,6},{137,8},{139,10},{141,12},{143,14}... | collective-permute-start | bytes 1572872 | tf_op jit(solution)/shard_map/ppermute | solution.py:32
  40.9 24.1 %collective-permute-start.3 = (bf16[2,8,128,128]{3,2,1,0:T(8,128)(2,1)S(1)}, bf16[2,8,128,128]{3,2,1,0:T(8,128)(2,1)S(1)}, u32[]{:S(2)}, u32[]{:S(2)}) collective-permute-start(bf16[2,8,128,128]{3,2,1,0:T(8,128)(2,1)S(1)} %get-tuple-element.14), channel_id=1, source_target_pairs={{1,0},{3,2},{5,4},{7,6},{9,8},{11,10},{13,12},{15,14},{17,16},{19,... | collective-permute-start | bytes 1572872 | tf_op jit(solution)/shard_map/ppermute | solution.py:32

commit v2 on v1

v2 whole, which is shorter than its diff:
```python
import functools
import math

import jax
import jax.numpy as jnp
from jax import lax
from jax.experimental import pallas as pl
from jax.experimental.pallas import tpu as pltpu
from jax.sharding import PartitionSpec as P

LOG2E = math.log2(math.e)
NN = (((1,), (0,)), ((), ()))
NT = (((1,), (1,)), ((), ()))
TN = (((0,), (0,)), ((), ()))
AXES = ("ctx", "head")
F32 = jnp.float32
BF16 = jnp.bfloat16
VMEM = pl.BlockSpec(memory_space=pltpu.VMEM)
SMEM = pl.BlockSpec(memory_space=pltpu.SMEM)
HBM = pl.BlockSpec(memory_space=pltpu.HBM)
CHUNKS = 2


def dot(a, b, dims):
    return lax.dot_general(a, b, dims, preferred_element_type=F32)


def route(x, pairs):
    far = lax.axis_size("ctx") // 2

    def device(role, c):
        return (c + (far if role[0] == "L" else 0)) * 2 + int(role[1])

    table = []
    for pair in pairs.split():
        src, dst = pair.split(">")
        table += [(device(src, c), device(dst, c)) for c in range(far)]
    return lax.ppermute(x, AXES, table)


def call(kernel, name, in_specs, out_specs, out_shape, scratch=(), aliases=None):
    return pl.pallas_call(
        kernel,
        in_specs=in_specs,
        out_specs=out_specs,
        out_shape=out_shape,
        scratch_shapes=list(scratch),
        input_output_aliases=aliases or {},
        compiler_params=pltpu.CompilerParams(vmem_limit_bytes=24 << 20),
        cost_estimate=pl.CostEstimate(flops=1, bytes_accessed=1 << 20, transcendentals=0),
        name=name,
    )


def group_grads(q_ref, g_ref, lse_ref, delta_ref, g, kvs, at, causal):
    rows, width = q_ref.shape[1:]
    ratio = 8
    lo = g * ratio
    scale = 1.0 / math.sqrt(width)
    q = q_ref[lo : lo + ratio].reshape(ratio * rows, width)
    g_out = g_ref[lo : lo + ratio].reshape(ratio * rows, width)
    base = lo // 16 * 16
    lse = lse_ref[base : base + 16].astype(F32)[lo - base : lo - base + ratio] * LOG2E
    delta = delta_ref[base : base + 16].astype(F32)[lo - base : lo - base + ratio]
    lse_row = jnp.concatenate([lse[i : i + 1, :] for i in range(ratio)], 1)
    delta_row = jnp.concatenate([delta[i : i + 1, :] for i in range(ratio)], 1)
    k = jnp.concatenate([r[0, at] for r in kvs], 0)
    v = jnp.concatenate([r[1, at] for r in kvs], 0)
    probs = jnp.exp2(dot(k, q, NT) * (scale * LOG2E) - lse_row)
    if causal:
        key = lax.broadcasted_iota(jnp.int32, probs.shape, 0)
        row = lax.broadcasted_iota(jnp.int32, probs.shape, 1) % rows
        probs = jnp.where(key <= row, probs, 0.0)
    dprobs = dot(v, g_out, NT)
    dscores = (probs * (dprobs - delta_row)).astype(BF16)
    dvalue = dot(probs.astype(BF16), g_out, NN)
    dkey = dot(dscores, q, NN) * scale
    dquery = dot(dscores, k, TN) * scale
    return dquery.reshape(ratio, rows, width), dkey, dvalue


def pack_kernel(flags, k_ref, v_ref, *refs):
    outs, sem = refs[:-1], refs[-1]
    copies = []
    for i, out in enumerate(outs):
        n = out.shape[1]
        for j, src in enumerate((k_ref, v_ref)):
            copies.append(pltpu.make_async_copy(src.at[pl.ds(i * n, n)], out.at[j], sem.at[2 * i + j]))
    for c in copies:
        c.start()
    for c in copies:
        c.wait()


def repeat(held, later):
    for src, out in zip(held, later):
        out[...] = src[...]


def load_kernel(q_hbm, g_hbm, lse_hbm, delta_hbm, *refs):
    n = (len(refs) - 5) // 2
    held, (q_ref, g_ref, lse_ref, delta_ref), later, sem = (
        refs[:n], refs[n : n + 4], refs[n + 4 : -1], refs[-1]
    )
    copies = [
        pltpu.make_async_copy(lse_hbm, lse_ref, sem.at[0]),
        pltpu.make_async_copy(delta_hbm, delta_ref, sem.at[1]),
    ]
    pieces = 4
    size = q_hbm.shape[0] // pieces
    for i in range(pieces):
        cut = pl.ds(i * size, size)
        copies.append(pltpu.make_async_copy(q_hbm.at[cut], q_ref.at[cut], sem.at[2 + 2 * i]))
        copies.append(pltpu.make_async_copy(g_hbm.at[cut], g_ref.at[cut], sem.at[3 + 2 * i]))
    for c in copies:
        c.start()
    repeat(held, later)
    for c in copies:
        c.wait()


def pair_kernel(first, flag_at, n_kv, n_held, n_after, with_sum, flags, q_ref, g_ref, lse_ref, delta_ref, *refs):
    refs = refs[n_after:]
    if with_sum:
        rx_ref, ry_ref, rz_ref, *refs = refs
        *refs, sum_ref = refs
        sum_ref[...] = rx_ref[...].astype(F32) + ry_ref[...].astype(F32) + rz_ref[...].astype(F32)
    kv_refs, refs = refs[:n_kv], refs[n_kv:]
    held, refs = refs[:n_held], refs[n_held:]
    dq_ref, outs, later = refs[0], refs[1 : 1 + n_kv], refs[1 + n_kv :]
    repeat(held, later)
    groups = kv_refs[0].shape[1]
    rows = q_ref.shape[1]
    ratio = 8

    @pl.when(flags[flag_at] == 1)
    def _():
        for i in range(groups):
            dq, dk, dv = group_grads(
                q_ref, g_ref, lse_ref, delta_ref, first + i, kv_refs, i, False
            )
            dq_ref[i * ratio : (i + 1) * ratio] = dq
            for j, out in enumerate(outs):
                out[0, i] = dk[j * rows : (j + 1) * rows].astype(BF16)
                out[1, i] = dv[j * rows : (j + 1) * rows].astype(BF16)


def diag_kernel(flags, q_ref, g_ref, lse_ref, delta_ref, *refs):
    parts, near_refs, far_refs = refs[0:2], refs[2:4], refs[4:6]
    dq_hbm, dkv_ref, dq_half, sem = refs[6:]
    n = parts[0].shape[1]
    ratio = 8
    stores = []
    has_near, has_far = flags[0] == 1, flags[1] == 1
    for g in range(2 * n):
        c, i = g // n, g % n
        dq, dk, dv = group_grads(q_ref, g_ref, lse_ref, delta_ref, g, [parts[c]], i, True)
        at = slice(g * ratio, (g + 1) * ratio)
        of = slice(i * ratio, (i + 1) * ratio)
        dq = dq + jnp.where(has_near, near_refs[c][of], 0.0)
        dq = dq + jnp.where(has_far, far_refs[c][of], 0.0)
        dq_half[at] = dq.astype(BF16)
        cut = pl.ds(g * ratio, ratio)
        stores.append(pltpu.make_async_copy(dq_half.at[cut], dq_hbm.at[cut], sem.at[g]))
        stores[-1].start()
        dkv_ref[0, g] = dk
        dkv_ref[1, g] = dv
    for c in stores:
        c.wait()


def final_kernel(dkv_ref, sum_ref, rx_ref, ry_ref, rz_ref, dk_hbm, dv_hbm, half, sem):
    n = rz_ref.shape[1]
    copies = []
    for j, out in enumerate((dk_hbm, dv_hbm)):
        half[j, :n] = (dkv_ref[j, :n] + sum_ref[j]).astype(BF16)
        far = rx_ref[j].astype(F32) + ry_ref[j].astype(F32)
        half[j, n:] = (dkv_ref[j, n:] + rz_ref[j].astype(F32) + far).astype(BF16)
        copies.append(pltpu.make_async_copy(half.at[j], out, sem.at[j]))
        copies[-1].start()
    for c in copies:
        c.wait()


def in_hbm(x):
    return pltpu.with_memory_space_constraint(x, pltpu.HBM)


def local(queries, keys, values, delta, grad_out, lse):
    half = lax.axis_index("head")
    is_late = lax.axis_index("ctx") >= lax.axis_size("ctx") // 2
    flags = jnp.stack([half.astype(jnp.int32), is_late.astype(jnp.int32)])
    heads, rows, width = queries.shape
    groups = keys.shape[0]
    n = groups // CHUNKS
    shape = jax.ShapeDtypeStruct
    part = shape((2, n, rows, width), BF16)
    dq_part = shape((heads // CHUNKS, rows, width), F32)
    sem = pltpu.SemaphoreType.DMA
    parts = call(
        pack_kernel, "pack", [SMEM] + [HBM] * 2, [VMEM] * CHUNKS, [part] * CHUNKS, [sem((2 * CHUNKS,))]
    )(flags, in_hbm(keys), in_hbm(values))

    up0, down0 = route(parts[0], "E0>L0 E1>L1 L0>E0"), route(parts[0], "E0>L1 E1>L0")
    *rows_in, later = call(
        load_kernel,
        "load",
        [HBM] * 4 + [VMEM],
        [VMEM] * 5,
        [shape(x.shape, BF16) for x in (queries, grad_out, lse, delta)] + [part],
        [sem((10,))],
    )(*(in_hbm(x) for x in (queries, grad_out, lse, delta)), parts[1])
    up1, down1 = route(later, "E0>L0 E1>L1 L0>E0"), route(later, "E0>L1 E1>L0")

    def to_second(x):
        return route(x, "E0>L1 L0>E1")

    def to_early(x, y):
        return route(x, "L0>E0 L1>E1"), route(y, "L1>E0 L0>E1")

    def pairs(name, flag_at, kvs, held=(), add=(), after=()):
        n_held, n_sum = len(held), len(add) // 3
        return call(
            functools.partial(
                pair_kernel, int(name[-1]) * n, flag_at, len(kvs), n_held, len(after), n_sum
            ),
            name,
            [SMEM] + [VMEM] * (4 + len(after) + len(kvs) + n_held + len(add)),
            [VMEM] * (1 + len(kvs) + n_held + n_sum),
            [dq_part] + [part] * (len(kvs) + n_held) + [shape(part.shape, F32)] * n_sum,
        )(flags, *rows_in, *after, *add, *kvs, *held)

    kv_near0 = to_second(up0)
    dq_far0, dx0, dy0 = pairs("far0", 1, [up0, down0])
    rx0, ry0 = to_early(dx0, dy0)
    dq_near0, dz0, mid1 = pairs("near0", 0, [kv_near0], held=[up1], after=[dq_far0])
    rz0 = route(dz0, "E1>E0 L1>L0")
    kv_near1 = to_second(mid1)
    dq_far1, dx1, dy1 = pairs("far1", 1, [up1, down1], after=[dq_near0])
    rx1, ry1 = to_early(dx1, dy1)
    dq_near1, dz1, far_sum = pairs("near1", 0, [kv_near1], add=[rx0, ry0, rz0], after=[dq_far1])
    rz1 = route(dz1, "E1>E0 L1>L0")
    whole = (2, groups, rows, width)
    dq, dkv = call(
        diag_kernel,
        "diag",
        [SMEM] + [VMEM] * 10,
        [HBM, VMEM],
        [shape(queries.shape, BF16), shape(whole, F32)],
        [pltpu.VMEM(queries.shape, BF16), sem((groups,))],
    )(flags, *rows_in, *parts, dq_near0, dq_near1, dq_far0, dq_far1)
    dk, dv = call(
        final_kernel,
        "final",
        [VMEM] * 5,
        [HBM] * 2,
        [shape(keys.shape, BF16)] * 2,
        [pltpu.VMEM(whole, BF16), sem((2,))],
    )(dkv, far_sum, rx1, ry1, rz1)
    return dq, dk, dv


def solution(mesh):
    spec3 = P(None, AXES, None)
    spec2 = P(None, AXES)
    return jax.shard_map(
        local,
        mesh=mesh,
        in_specs=(spec3, spec3, spec3, spec2, spec3, spec2),
        out_specs=(spec3, spec3, spec3),
        check_vma=False,
    )
```

time: 66.4 us -> 49.8 us (0.75)
  the two profiles are of different devices: /device:TPU:42 before, /device:TPU:72 now
where the time goes in v2:
time: 49.8 us; the launch traced here: 49.1 us
  starting transfers between devices  29.3 us (59%)
  Pallas kernels  11.8 us (24%)
  waiting for transfers between devices  6.96 us (14%)
  between operations  1.01 us (2%)
    ppermute x12, starting transfers between devices, route(): return lax.ppermute(x, AXES, table)  29.3 us
    ppermute x12, waiting for transfers between devices, route(): return lax.ppermute(x, AXES, table)  6.96 us
    pallas_call x1, Pallas kernels, local(): call(diag_kernel, 'diag', [SMEM] + [VMEM] * 10, [HBM, VMEM], [shape(queri...  4.67 us
    pallas_call x4, Pallas kernels, pairs(): call(functools.partial(pair_kernel, int(name[-1]) * n, flag_at, len(kvs),...  2.29 us
    pallas_call x1, Pallas kernels, local(): call(load_kernel, 'load', [HBM] * 4 + [VMEM], [VMEM] * 5, [shape(x.shape,...  2.27 us
    pallas_call x1, Pallas kernels, local(): call(pack_kernel, 'pack', [SMEM] + [HBM] * 2, [VMEM] * CHUNKS, [part] * C...  1.67 us
  transfers between devices with their start and end apart: 12, of which 3 were waited for; matrix products, arithmetic and copies ran while one was open for 0% of the time, Pallas kernels for 19%

profile of v2, /device:TPU:72, one launch (start us, length us, event | category | flops | bytes accessed | tf_op | source)
XLA Modules:
  0.0 49.1 jit_solution(2977788342545359878)
XLA Ops:
  0.6 0.1 pad_add_fusion.flags
  0.7 1.7 %pack.1 = (bf16[2,4,128,128]{3,2,1,0:T(8,128)(2,1)S(1)}, bf16[2,4,128,128]{3,2,1,0:T(8,128)(2,1)S(1)}) custom-call(s32[2]{0:T(128)S(1)} %pad_add_fusion.flags, bf16[8,128,128]{2,1,0:T(8,128)(2,1)} %k_ref.1, bf16[8,128,128]{2,1,0:T(8,128)(2,1)} %v_ref.1), custom_call_target="tpu_custom_call" | custom-call | flops 1 | bytes 1048576 | tf_op jit(solution)/shard_map/pack/pallas_call | solution.py:200
  2.4 3.4 %collective-permute-start = (bf16[2,4,128,128]{3,2,1,0:T(8,128)(2,1)S(1)}, bf16[2,4,128,128]{3,2,1,0:T(8,128)(2,1)S(1)}, u32[]{:S(2)}, u32[]{:S(2)}) collective-permute-start(bf16[2,4,128,128]{3,2,1,0:T(8,128)(2,1)S(1)} %get-tuple-element.31.refs_0_), channel_id=1, source_target_pairs={{0,128},{2,130},{4,132},{6,134},{8,136},{10,138},{12,140},{14,142}... | collective-permute-start | bytes 786440 | tf_op jit(solution)/shard_map/ppermute | solution.py:38
  5.8 2.6 %collective-permute-start.1 = (bf16[2,4,128,128]{3,2,1,0:T(8,128)(2,1)S(1)}, bf16[2,4,128,128]{3,2,1,0:T(8,128)(2,1)S(1)}, u32[]{:S(2)}, u32[]{:S(2)}) collective-permute-start(bf16[2,4,128,128]{3,2,1,0:T(8,128)(2,1)S(1)} %get-tuple-element.31.refs_0_), channel_id=1, source_target_pairs={{0,129},{2,131},{4,133},{6,135},{8,137},{10,139},{12,141},{14,143}... | collective-permute-start | bytes 786440 | tf_op jit(solution)/shard_map/ppermute | solution.py:38
  8.4 2.3 %load.1 = (bf16[64,128,128]{2,1,0:T(8,128)(2,1)S(1)}, bf16[64,128,128]{2,1,0:T(8,128)(2,1)S(1)}, bf16[64,128]{1,0:T(8,128)(2,1)S(1)}, bf16[64,128]{1,0:T(8,128)(2,1)S(1)}, bf16[2,4,128,128]{3,2,1,0:T(8,128)(2,1)S(1)}) custom-call(bf16[64,128,128]{2,1,0:T(8,128)(2,1)} %q_hbm.1, bf16[64,128,128]{2,1,0:T(8,128)(2,1)} %g_hbm.1, bf16[64,128]{1,0:T(8,128)(2,1)} %lse_hbm.1, ...), custom_call_target="tpu_custom_call" | custom-call | flops 1 | bytes 1048576 | tf_op jit(solution)/shard_map/load/pallas_call | solution.py:205
  10.7 1.9 %collective-permute-start.3 = (bf16[2,4,128,128]{3,2,1,0:T(8,128)(2,1)S(1)}, bf16[2,4,128,128]{3,2,1,0:T(8,128)(2,1)S(1)}, u32[]{:S(2)}, u32[]{:S(2)}) collective-permute-start(bf16[2,4,128,128]{3,2,1,0:T(8,128)(2,1)S(1)} %get-tuple-element.33), channel_id=1, source_target_pairs={{0,128},{2,130},{4,132},{6,134},{8,136},{10,138},{12,140},{14,142}... | collective-permute-start | bytes 786440 | tf_op jit(solution)/shard_map/ppermute | solution.py:38
  12.6 0.0 collective-permute-done.refs_0_
  12.6 4.9 %collective-permute-start.2 = (bf16[2,4,128,128]{3,2,1,0:T(8,128)(2,1)S(1)}, bf16[2,4,128,128]{3,2,1,0:T(8,128)(2,1)S(1)}, u32[]{:S(2)}, u32[]{:S(2)}) collective-permute-start(bf16[2,4,128,128]{3,2,1,0:T(8,128)(2,1)S(1)} %collective-permute-done.refs_0_), channel_id=1, source_target_pairs={{0,129},{2,131},{4,133},{6,135},{8,137},{10,139},{12,141},{14,143}... | collective-permute-start | bytes 786440 | tf_op jit(solution)/shard_map/ppermute | solution.py:38
  17.5 1.3 %collective-permute-start.4 = (bf16[2,4,128,128]{3,2,1,0:T(8,128)(2,1)S(1)}, bf16[2,4,128,128]{3,2,1,0:T(8,128)(2,1)S(1)}, u32[]{:S(2)}, u32[]{:S(2)}) collective-permute-start(bf16[2,4,128,128]{3,2,1,0:T(8,128)(2,1)S(1)} %get-tuple-element.33), channel_id=1, source_target_pairs={{0,129},{2,131},{4,133},{6,135},{8,137},{10,139},{12,141},{14,143}... | collective-permute-start | bytes 786440 | tf_op jit(solution)/shard_map/ppermute | solution.py:38
  18.8 0.0 collective-permute-done.1.refs_1_
  18.8 0.6 %far0.1 = (f32[32,128,128]{2,1,0:T(8,128)S(1)}, bf16[2,4,128,128]{3,2,1,0:T(8,128)(2,1)S(1)}, bf16[2,4,128,128]{3,2,1,0:T(8,128)(2,1)S(1)}) custom-call(s32[2]{0:T(128)S(1)} %pad_add_fusion.flags, bf16[64,128,128]{2,1,0:T(8,128)(2,1)S(1)} %get-tuple-element.27.q_ref, bf16[64,128,128]{2,1,0:T(8,128)(2,1)S(1)} %get-tuple-element.28.g_ref, ...), custom_call_target="tpu_custom_call" | custom-call | flops 1 | bytes 1048576 | tf_op jit(solution)/shard_map/far0/pallas_call | solution.py:223
  19.3 1.3 %collective-permute-start.5 = (bf16[2,4,128,128]{3,2,1,0:T(8,128)(2,1)S(1)}, bf16[2,4,128,128]{3,2,1,0:T(8,128)(2,1)S(1)}, u32[]{:S(2)}, u32[]{:S(2)}) collective-permute-start(bf16[2,4,128,128]{3,2,1,0:T(8,128)(2,1)S(1)} %get-tuple-element.36), channel_id=1, source_target_pairs={{128,0},{130,2},{132,4},{134,6},{136,8},{138,10},{140,12},{142,14}... | collective-permute-start | bytes 786440 | tf_op jit(solution)/shard_map/ppermute | solution.py:38
  20.6 1.3 %collective-permute-start.6 = (bf16[2,4,128,128]{3,2,1,0:T(8,128)(2,1)S(1)}, bf16[2,4,128,128]{3,2,1,0:T(8,128)(2,1)S(1)}, u32[]{:S(2)}, u32[]{:S(2)}) collective-permute-start(bf16[2,4,128,128]{3,2,1,0:T(8,128)(2,1)S(1)} %get-tuple-element.37), channel_id=1, source_target_pairs={{129,0},{131,2},{133,4},{135,6},{137,8},{139,10},{141,12},{143,14}... | collective-permute-start | bytes 786440 | tf_op jit(solution)/shard_map/ppermute | solution.py:38
  21.9 0.0 collective-permute-done.3.refs_2_.refs_1_
  21.9 2.2 %collective-permute-done.2.refs_1_ = bf16[2,4,128,128]{3,2,1,0:T(8,128)(2,1)S(1)} collective-permute-done((bf16[2,4,128,128]{3,2,1,0:T(8,128)(2,1)S(1)}, bf16[2,4,128,128]{3,2,1,0:T(8,128)(2,1)S(1)}, u32[]{:S(2)}, u32[]{:S(2)}) %collective-permute-start.2) | collective-permute-done | bytes 262176 | tf_op jit(solution)/shard_map/ppermute | solution.py:38
  24.2 0.6 %near0.1 = (f32[32,128,128]{2,1,0:T(8,128)S(1)}, bf16[2,4,128,128]{3,2,1,0:T(8,128)(2,1)S(1)}, bf16[2,4,128,128]{3,2,1,0:T(8,128)(2,1)S(1)}) custom-call(s32[2]{0:T(128)S(1)} %pad_add_fusion.flags, bf16[64,128,128]{2,1,0:T(8,128)(2,1)S(1)} %get-tuple-element.27.q_ref, bf16[64,128,128]{2,1,0:T(8,128)(2,1)S(1)} %get-tuple-element.28.g_ref, ...), custom_call_target="tpu_custom_call" | custom-call | flops 1 | bytes 1048576 | tf_op jit(solution)/shard_map/near0/pallas_call | solution.py:223
  24.7 1.3 %collective-permute-start.7 = (bf16[2,4,128,128]{3,2,1,0:T(8,128)(2,1)S(1)}, bf16[2,4,128,128]{3,2,1,0:T(8,128)(2,1)S(1)}, u32[]{:S(2)}, u32[]{:S(2)}) collective-permute-start(bf16[2,4,128,128]{3,2,1,0:T(8,128)(2,1)S(1)} %get-tuple-element.38), channel_id=1, source_target_pairs={{1,0},{3,2},{5,4},{7,6},{9,8},{11,10},{13,12},{15,14},{17,16},{19,... | collective-permute-start | bytes 786440 | tf_op jit(solution)/shard_map/ppermute | solution.py:38
  26.0 7.3 %collective-permute-start.8 = (bf16[2,4,128,128]{3,2,1,0:T(8,128)(2,1)S(1)}, bf16[2,4,128,128]{3,2,1,0:T(8,128)(2,1)S(1)}, u32[]{:S(2)}, u32[]{:S(2)}) collective-permute-start(bf16[2,4,128,128]{3,2,1,0:T(8,128)(2,1)S(1)} %get-tuple-element.39), channel_id=1, source_target_pairs={{0,129},{2,131},{4,133},{6,135},{8,137},{10,139},{12,141},{14,143}... | collective-permute-start | bytes 786440 | tf_op jit(solution)/shard_map/ppermute | solution.py:38
  33.4 0.0 collective-permute-done.4.refs_2_
  33.4 0.6 %far1.1 = (f32[32,128,128]{2,1,0:T(8,128)S(1)}, bf16[2,4,128,128]{3,2,1,0:T(8,128)(2,1)S(1)}, bf16[2,4,128,128]{3,2,1,0:T(8,128)(2,1)S(1)}) custom-call(s32[2]{0:T(128)S(1)} %pad_add_fusion.flags, bf16[64,128,128]{2,1,0:T(8,128)(2,1)S(1)} %get-tuple-element.27.q_ref, bf16[64,128,128]{2,1,0:T(8,128)(2,1)S(1)} %get-tuple-element.28.g_ref, ...), custom_call_target="tpu_custom_call" | custom-call | flops 1 | bytes 1048576 | tf_op jit(solution)/shard_map/far1/pallas_call | solution.py:223
  33.9 1.3 %collective-permute-start.9 = (bf16[2,4,128,128]{3,2,1,0:T(8,128)(2,1)S(1)}, bf16[2,4,128,128]{3,2,1,0:T(8,128)(2,1)S(1)}, u32[]{:S(2)}, u32[]{:S(2)}) collective-permute-start(bf16[2,4,128,128]{3,2,1,0:T(8,128)(2,1)S(1)} %get-tuple-element.44), channel_id=1, source_target_pairs={{128,0},{130,2},{132,4},{134,6},{136,8},{138,10},{140,12},{142,14}... | collective-permute-start | bytes 786440 | tf_op jit(solution)/shard_map/ppermute | solution.py:38
  35.2 0.0 collective-permute-done.5.refs_1_
  35.2 1.3 %collective-permute-start.10 = (bf16[2,4,128,128]{3,2,1,0:T(8,128)(2,1)S(1)}, bf16[2,4,128,128]{3,2,1,0:T(8,128)(2,1)S(1)}, u32[]{:S(2)}, u32[]{:S(2)}) collective-permute-start(bf16[2,4,128,128]{3,2,1,0:T(8,128)(2,1)S(1)} %get-tuple-element.45), channel_id=1, source_target_pairs={{129,0},{131,2},{133,4},{135,6},{137,8},{139,10},{141,12},{143,14}... | collective-permute-start | bytes 786440 | tf_op jit(solution)/shard_map/ppermute | solution.py:38
  36.5 0.0 collective-permute-done.6.refs_2_
  36.5 0.0 collective-permute-done.7.refs_3_
  36.6 0.7 %collective-permute-done.8.refs_4_ = bf16[2,4,128,128]{3,2,1,0:T(8,128)(2,1)S(1)} collective-permute-done((bf16[2,4,128,128]{3,2,1,0:T(8,128)(2,1)S(1)}, bf16[2,4,128,128]{3,2,1,0:T(8,128)(2,1)S(1)}, u32[]{:S(2)}, u32[]{:S(2)}) %collective-permute-start.8) | collective-permute-done | bytes 262176 | tf_op jit(solution)/shard_map/ppermute | solution.py:38
  37.2 0.6 %near1.1 = (f32[32,128,128]{2,1,0:T(8,128)S(1)}, bf16[2,4,128,128]{3,2,1,0:T(8,128)(2,1)S(1)}, f32[2,4,128,128]{3,2,1,0:T(8,128)S(1)}) custom-call(s32[2]{0:T(128)S(1)} %pad_add_fusion.flags, bf16[64,128,128]{2,1,0:T(8,128)(2,1)S(1)} %get-tuple-element.27.q_ref, bf16[64,128,128]{2,1,0:T(8,128)(2,1)S(1)} %get-tuple-element.28.g_ref, ...), custom_call_target="tpu_custom_call" | custom-call | flops 1 | bytes 1048576 | tf_op jit(solution)/shard_map/near1/pallas_call | solution.py:223
  37.8 1.5 %collective-permute-start.11 = (bf16[2,4,128,128]{3,2,1,0:T(8,128)(2,1)S(1)}, bf16[2,4,128,128]{3,2,1,0:T(8,128)(2,1)S(1)}, u32[]{:S(2)}, u32[]{:S(2)}) collective-permute-start(bf16[2,4,128,128]{3,2,1,0:T(8,128)(2,1)S(1)} %get-tuple-element.46), channel_id=1, source_target_pairs={{1,0},{3,2},{5,4},{7,6},{9,8},{11,10},{13,12},{15,14},{17,16},{19,... | collective-permute-start | bytes 786440 | tf_op jit(solution)/shard_map/ppermute | solution.py:38
  39.3 4.7 %diag.1 = (bf16[64,128,128]{2,1,0:T(8,128)(2,1)}, f32[2,8,128,128]{3,2,1,0:T(8,128)S(1)}) custom-call(s32[2]{0:T(128)S(1)} %pad_add_fusion.flags, bf16[64,128,128]{2,1,0:T(8,128)(2,1)S(1)} %get-tuple-element.27.q_ref, bf16[64,128,128]{2,1,0:T(8,128)(2,1)S(1)} %get-tuple-element.28.g_ref, bf16[64,128]{1,0:T(8,128)(2,1)S(1)} %get-tuple-element.29.lse_ref, ...), custom_call_target="tpu_custom_call" | custom-call | flops 1 | bytes 1048576 | tf_op jit(solution)/shard_map/diag/pallas_call | solution.py:244
  44.0 0.0 collective-permute-done.9.rx_ref
  44.0 4.0 %collective-permute-done.10.ry_ref = bf16[2,4,128,128]{3,2,1,0:T(8,128)(2,1)S(1)} collective-permute-done((bf16[2,4,128,128]{3,2,1,0:T(8,128)(2,1)S(1)}, bf16[2,4,128,128]{3,2,1,0:T(8,128)(2,1)S(1)}, u32[]{:S(2)}, u32[]{:S(2)}) %collective-permute-start.10) | collective-permute-done | bytes 262176 | tf_op jit(solution)/shard_map/ppermute | solution.py:38
  48.1 0.0 collective-permute-done.11.rz_ref
  48.1 0.9 %final.1 = (bf16[8,128,128]{2,1,0:T(8,128)(2,1)}, bf16[8,128,128]{2,1,0:T(8,128)(2,1)}) custom-call(f32[2,8,128,128]{3,2,1,0:T(8,128)S(1)} %get-tuple-element.42.dkv_ref, f32[2,4,128,128]{3,2,1,0:T(8,128)S(1)} %get-tuple-element.43.sum_ref, bf16[2,4,128,128]{3,2,1,0:T(8,128)(2,1)S(1)} %collective-permute-done.9.rx_ref, ...), custom_call_target="tpu_custom_call" | custom-call | flops 1 | bytes 1048576 | tf_op jit(solution)/shard_map/final/pallas_call | solution.py:252
Async XLA Ops:
  2.4 10.2 %collective-permute-start = (bf16[2,4,128,128]{3,2,1,0:T(8,128)(2,1)S(1)}, bf16[2,4,128,128]{3,2,1,0:T(8,128)(2,1)S(1)}, u32[]{:S(2)}, u32[]{:S(2)}) collective-permute-start(bf16[2,4,128,128]{3,2,1,0:T(8,128)(2,1)S(1)} %get-tuple-element.31.refs_0_), channel_id=1, source_target_pairs={{0,128},{2,130},{4,132},{6,134},{8,136},{10,138},{12,140},{14,142}... | collective-permute-start | bytes 786440 | tf_op jit(solution)/shard_map/ppermute | solution.py:38
  5.8 13.0 %collective-permute-start.1 = (bf16[2,4,128,128]{3,2,1,0:T(8,128)(2,1)S(1)}, bf16[2,4,128,128]{3,2,1,0:T(8,128)(2,1)S(1)}, u32[]{:S(2)}, u32[]{:S(2)}) collective-permute-start(bf16[2,4,128,128]{3,2,1,0:T(8,128)(2,1)S(1)} %get-tuple-element.31.refs_0_), channel_id=1, source_target_pairs={{0,129},{2,131},{4,133},{6,135},{8,137},{10,139},{12,141},{14,143}... | collective-permute-start | bytes 786440 | tf_op jit(solution)/shard_map/ppermute | solution.py:38
  10.7 11.3 %collective-permute-start.3 = (bf16[2,4,128,128]{3,2,1,0:T(8,128)(2,1)S(1)}, bf16[2,4,128,128]{3,2,1,0:T(8,128)(2,1)S(1)}, u32[]{:S(2)}, u32[]{:S(2)}) collective-permute-start(bf16[2,4,128,128]{3,2,1,0:T(8,128)(2,1)S(1)} %get-tuple-element.33), channel_id=1, source_target_pairs={{0,128},{2,130},{4,132},{6,134},{8,136},{10,138},{12,140},{14,142}... | collective-permute-start | bytes 786440 | tf_op jit(solution)/shard_map/ppermute | solution.py:38
  12.6 11.6 %collective-permute-start.2 = (bf16[2,4,128,128]{3,2,1,0:T(8,128)(2,1)S(1)}, bf16[2,4,128,128]{3,2,1,0:T(8,128)(2,1)S(1)}, u32[]{:S(2)}, u32[]{:S(2)}) collective-permute-start(bf16[2,4,128,128]{3,2,1,0:T(8,128)(2,1)S(1)} %collective-permute-done.refs_0_), channel_id=1, source_target_pairs={{0,129},{2,131},{4,133},{6,135},{8,137},{10,139},{12,141},{14,143}... | collective-permute-start | bytes 786440 | tf_op jit(solution)/shard_map/ppermute | solution.py:38
  17.5 15.9 %collective-permute-start.4 = (bf16[2,4,128,128]{3,2,1,0:T(8,128)(2,1)S(1)}, bf16[2,4,128,128]{3,2,1,0:T(8,128)(2,1)S(1)}, u32[]{:S(2)}, u32[]{:S(2)}) collective-permute-start(bf16[2,4,128,128]{3,2,1,0:T(8,128)(2,1)S(1)} %get-tuple-element.33), channel_id=1, source_target_pairs={{0,129},{2,131},{4,133},{6,135},{8,137},{10,139},{12,141},{14,143}... | collective-permute-start | bytes 786440 | tf_op jit(solution)/shard_map/ppermute | solution.py:38
  19.3 15.9 %collective-permute-start.5 = (bf16[2,4,128,128]{3,2,1,0:T(8,128)(2,1)S(1)}, bf16[2,4,128,128]{3,2,1,0:T(8,128)(2,1)S(1)}, u32[]{:S(2)}, u32[]{:S(2)}) collective-permute-start(bf16[2,4,128,128]{3,2,1,0:T(8,128)(2,1)S(1)} %get-tuple-element.36), channel_id=1, source_target_pairs={{128,0},{130,2},{132,4},{134,6},{136,8},{138,10},{140,12},{142,14}... | collective-permute-start | bytes 786440 | tf_op jit(solution)/shard_map/ppermute | solution.py:38
  20.6 15.9 %collective-permute-start.6 = (bf16[2,4,128,128]{3,2,1,0:T(8,128)(2,1)S(1)}, bf16[2,4,128,128]{3,2,1,0:T(8,128)(2,1)S(1)}, u32[]{:S(2)}, u32[]{:S(2)}) collective-permute-start(bf16[2,4,128,128]{3,2,1,0:T(8,128)(2,1)S(1)} %get-tuple-element.37), channel_id=1, source_target_pairs={{129,0},{131,2},{133,4},{135,6},{137,8},{139,10},{141,12},{143,14}... | collective-permute-start | bytes 786440 | tf_op jit(solution)/shard_map/ppermute | solution.py:38
  24.7 11.8 %collective-permute-start.7 = (bf16[2,4,128,128]{3,2,1,0:T(8,128)(2,1)S(1)}, bf16[2,4,128,128]{3,2,1,0:T(8,128)(2,1)S(1)}, u32[]{:S(2)}, u32[]{:S(2)}) collective-permute-start(bf16[2,4,128,128]{3,2,1,0:T(8,128)(2,1)S(1)} %get-tuple-element.38), channel_id=1, source_target_pairs={{1,0},{3,2},{5,4},{7,6},{9,8},{11,10},{13,12},{15,14},{17,16},{19,... | collective-permute-start | bytes 786440 | tf_op jit(solution)/shard_map/ppermute | solution.py:38
  26.0 11.2 %collective-permute-start.8 = (bf16[2,4,128,128]{3,2,1,0:T(8,128)(2,1)S(1)}, bf16[2,4,128,128]{3,2,1,0:T(8,128)(2,1)S(1)}, u32[]{:S(2)}, u32[]{:S(2)}) collective-permute-start(bf16[2,4,128,128]{3,2,1,0:T(8,128)(2,1)S(1)} %get-tuple-element.39), channel_id=1, source_target_pairs={{0,129},{2,131},{4,133},{6,135},{8,137},{10,139},{12,141},{14,143}... | collective-permute-start | bytes 786440 | tf_op jit(solution)/shard_map/ppermute | solution.py:38
  33.9 10.1 %collective-permute-start.9 = (bf16[2,4,128,128]{3,2,1,0:T(8,128)(2,1)S(1)}, bf16[2,4,128,128]{3,2,1,0:T(8,128)(2,1)S(1)}, u32[]{:S(2)}, u32[]{:S(2)}) collective-permute-start(bf16[2,4,128,128]{3,2,1,0:T(8,128)(2,1)S(1)} %get-tuple-element.44), channel_id=1, source_target_pairs={{128,0},{130,2},{132,4},{134,6},{136,8},{138,10},{140,12},{142,14}... | collective-permute-start | bytes 786440 | tf_op jit(solution)/shard_map/ppermute | solution.py:38
  35.2 12.8 %collective-permute-start.10 = (bf16[2,4,128,128]{3,2,1,0:T(8,128)(2,1)S(1)}, bf16[2,4,128,128]{3,2,1,0:T(8,128)(2,1)S(1)}, u32[]{:S(2)}, u32[]{:S(2)}) collective-permute-start(bf16[2,4,128,128]{3,2,1,0:T(8,128)(2,1)S(1)} %get-tuple-element.45), channel_id=1, source_target_pairs={{129,0},{131,2},{133,4},{135,6},{137,8},{139,10},{141,12},{143,14}... | collective-permute-start | bytes 786440 | tf_op jit(solution)/shard_map/ppermute | solution.py:38
  37.8 10.2 %collective-permute-start.11 = (bf16[2,4,128,128]{3,2,1,0:T(8,128)(2,1)S(1)}, bf16[2,4,128,128]{3,2,1,0:T(8,128)(2,1)S(1)}, u32[]{:S(2)}, u32[]{:S(2)}) collective-permute-start(bf16[2,4,128,128]{3,2,1,0:T(8,128)(2,1)S(1)} %get-tuple-element.46), channel_id=1, source_target_pairs={{1,0},{3,2},{5,4},{7,6},{9,8},{11,10},{13,12},{15,14},{17,16},{19,... | collective-permute-start | bytes 786440 | tf_op jit(solution)/shard_map/ppermute | solution.py:38

commit v3 on v2

--- a/solution.py
+++ b/solution.py
@@ -16,7 +16,6 @@
 F32 = jnp.float32
 BF16 = jnp.bfloat16
 VMEM = pl.BlockSpec(memory_space=pltpu.VMEM)
-SMEM = pl.BlockSpec(memory_space=pltpu.SMEM)
 HBM = pl.BlockSpec(memory_space=pltpu.HBM)
 CHUNKS = 2
 
@@ -79,7 +78,7 @@
     return dquery.reshape(ratio, rows, width), dkey, dvalue
 
 
-def pack_kernel(flags, k_ref, v_ref, *refs):
+def pack_kernel(k_ref, v_ref, *refs):
     outs, sem = refs[:-1], refs[-1]
     copies = []
     for i, out in enumerate(outs):
@@ -119,7 +118,7 @@
         c.wait()
 
 
-def pair_kernel(first, flag_at, n_kv, n_held, n_after, with_sum, flags, q_ref, g_ref, lse_ref, delta_ref, *refs):
+def pair_kernel(first, flag_at, n_kv, n_held, n_after, with_sum, q_ref, g_ref, lse_ref, delta_ref, *refs):
     refs = refs[n_after:]
     if with_sum:
         rx_ref, ry_ref, rz_ref, *refs = refs
@@ -133,7 +132,7 @@
     rows = q_ref.shape[1]
     ratio = 8
 
-    @pl.when(flags[flag_at] == 1)
+    @pl.when(is_late() if flag_at else is_second())
     def _():
         for i in range(groups):
             dq, dk, dv = group_grads(
@@ -145,13 +144,13 @@
                 out[1, i] = dv[j * rows : (j + 1) * rows].astype(BF16)
 
 
-def diag_kernel(flags, q_ref, g_ref, lse_ref, delta_ref, *refs):
+def diag_kernel(q_ref, g_ref, lse_ref, delta_ref, *refs):
     parts, near_refs, far_refs = refs[0:2], refs[2:4], refs[4:6]
     dq_hbm, dkv_ref, dq_half, sem = refs[6:]
     n = parts[0].shape[1]
     ratio = 8
     stores = []
-    has_near, has_far = flags[0] == 1, flags[1] == 1
+    has_near, has_far = is_second(), is_late()
     for g in range(2 * n):
         c, i = g // n, g % n
         dq, dk, dv = group_grads(q_ref, g_ref, lse_ref, delta_ref, g, [parts[c]], i, True)
@@ -182,14 +181,19 @@
         c.wait()
 
 
+def is_second():
+    return lax.axis_index("head") == 1
+
+
+def is_late():
+    return lax.axis_index("ctx") >= lax.axis_size("ctx") // 2
+
+
 def in_hbm(x):
     return pltpu.with_memory_space_constraint(x, pltpu.HBM)
 
 
 def local(queries, keys, values, delta, grad_out, lse):
-    half = lax.axis_index("head")
-    is_late = lax.axis_index("ctx") >= lax.axis_size("ctx") // 2
-    flags = jnp.stack([half.astype(jnp.int32), is_late.astype(jnp.int32)])
     heads, rows, width = queries.shape
     groups = keys.shape[0]
     n = groups // CHUNKS
@@ -198,8 +202,8 @@
     dq_part = shape((heads // CHUNKS, rows, width), F32)
     sem = pltpu.SemaphoreType.DMA
     parts = call(
-        pack_kernel, "pack", [SMEM] + [HBM] * 2, [VMEM] * CHUNKS, [part] * CHUNKS, [sem((2 * CHUNKS,))]
-    )(flags, in_hbm(keys), in_hbm(values))
+        pack_kernel, "pack", [HBM] * 2, [VMEM] * CHUNKS, [part] * CHUNKS, [sem((2 * CHUNKS,))]
+    )(in_hbm(keys), in_hbm(values))
 
     up0, down0 = route(parts[0], "E0>L0 E1>L1 L0>E0"), route(parts[0], "E0>L1 E1>L0")
     *rows_in, later = call(
@@ -225,10 +229,10 @@
                 pair_kernel, int(name[-1]) * n, flag_at, len(kvs), n_held, len(after), n_sum
             ),
             name,
-            [SMEM] + [VMEM] * (4 + len(after) + len(kvs) + n_held + len(add)),
+            [VMEM] * (4 + len(after) + len(kvs) + n_held + len(add)),
             [VMEM] * (1 + len(kvs) + n_held + n_sum),
             [dq_part] + [part] * (len(kvs) + n_held) + [shape(part.shape, F32)] * n_sum,
-        )(flags, *rows_in, *after, *add, *kvs, *held)
+        )(*rows_in, *after, *add, *kvs, *held)
 
     kv_near0 = to_second(up0)
     dq_far0, dx0, dy0 = pairs("far0", 1, [up0, down0])
@@ -244,11 +248,11 @@
     dq, dkv = call(
         diag_kernel,
         "diag",
-        [SMEM] + [VMEM] * 10,
+        [VMEM] * 10,
         [HBM, VMEM],
         [shape(queries.shape, BF16), shape(whole, F32)],
         [pltpu.VMEM(queries.shape, BF16), sem((groups,))],
-    )(flags, *rows_in, *parts, dq_near0, dq_near1, dq_far0, dq_far1)
+    )(*rows_in, *parts, dq_near0, dq_near1, dq_far0, dq_far1)
     dk, dv = call(
         final_kernel,
         "final",

time: 49.8 us -> 48.1 us (0.966)
  Pallas kernels: 11.8 us -> 8.46 us
  waiting for transfers between devices: 6.96 us -> 8.89 us
    pallas_call x4, Pallas kernels: 2.29 us -> 0.14 us  [pairs(): call(functools.partial(pair_kernel, int(name[-1]) * n, flag_at, len(kvs),...]
    ppermute x12, waiting for transfers between devices: 6.96 us -> 8.89 us  [route(): return lax.ppermute(x, AXES, table)]
    pallas_call x2, Pallas kernels: 6.33 us -> 5.16 us  [the longest x1 4.03 us: local(): call(diag_kernel, 'diag', [VMEM] * 10, [HBM, VMEM], [shape(queries.shape,...]
  transfers between devices with their start and end apart: 12 -> 12, of which waited for: 3 -> 4; matrix products, arithmetic and copies ran while one was open for 0% -> 0% of each run, Pallas kernels for 19% -> 14%
where the time goes in v3:
time: 48.1 us; the launch traced here: 47.6 us
  starting transfers between devices  29.3 us (61%)
  waiting for transfers between devices  8.89 us (18%)
  Pallas kernels  8.46 us (18%)
  between operations  1 us (2%)
    ppermute x12, starting transfers between devices, route(): return lax.ppermute(x, AXES, table)  29.3 us
    ppermute x12, waiting for transfers between devices, route(): return lax.ppermute(x, AXES, table)  8.89 us
    pallas_call x1, Pallas kernels, local(): call(diag_kernel, 'diag', [VMEM] * 10, [HBM, VMEM], [shape(queries.shape,...  4.03 us
    pallas_call x1, Pallas kernels, local(): call(load_kernel, 'load', [HBM] * 4 + [VMEM], [VMEM] * 5, [shape(x.shape,...  2.27 us
    pallas_call x1, Pallas kernels, local(): call(pack_kernel, 'pack', [HBM] * 2, [VMEM] * CHUNKS, [part] * CHUNKS, [s...  1.13 us
  transfers between devices with their start and end apart: 12, of which 4 were waited for; matrix products, arithmetic and copies ran while one was open for 0% of the time, Pallas kernels for 14%

profile of v3, /device:TPU:72, one launch (start us, length us, event | category | flops | bytes accessed | tf_op | source)
XLA Modules:
  0.0 47.6 jit_solution(4468219555288879483)
XLA Ops:
  0.6 1.1 %pack.1 = (bf16[2,4,128,128]{3,2,1,0:T(8,128)(2,1)S(1)}, bf16[2,4,128,128]{3,2,1,0:T(8,128)(2,1)S(1)}) custom-call(bf16[8,128,128]{2,1,0:T(8,128)(2,1)} %k_ref.1, bf16[8,128,128]{2,1,0:T(8,128)(2,1)} %v_ref.1), custom_call_target="tpu_custom_call" | custom-call | flops 1 | bytes 1048576 | tf_op jit(solution)/shard_map/pack/pallas_call | solution.py:204
  1.8 3.4 %collective-permute-start = (bf16[2,4,128,128]{3,2,1,0:T(8,128)(2,1)S(1)}, bf16[2,4,128,128]{3,2,1,0:T(8,128)(2,1)S(1)}, u32[]{:S(2)}, u32[]{:S(2)}) collective-permute-start(bf16[2,4,128,128]{3,2,1,0:T(8,128)(2,1)S(1)} %get-tuple-element.31.refs_0_), channel_id=1, source_target_pairs={{0,128},{2,130},{4,132},{6,134},{8,136},{10,138},{12,140},{14,142}... | collective-permute-start | bytes 786440 | tf_op jit(solution)/shard_map/ppermute | solution.py:37
  5.2 2.6 %collective-permute-start.1 = (bf16[2,4,128,128]{3,2,1,0:T(8,128)(2,1)S(1)}, bf16[2,4,128,128]{3,2,1,0:T(8,128)(2,1)S(1)}, u32[]{:S(2)}, u32[]{:S(2)}) collective-permute-start(bf16[2,4,128,128]{3,2,1,0:T(8,128)(2,1)S(1)} %get-tuple-element.31.refs_0_), channel_id=1, source_target_pairs={{0,129},{2,131},{4,133},{6,135},{8,137},{10,139},{12,141},{14,143}... | collective-permute-start | bytes 786440 | tf_op jit(solution)/shard_map/ppermute | solution.py:37
  7.8 2.3 %load.1 = (bf16[64,128,128]{2,1,0:T(8,128)(2,1)S(1)}, bf16[64,128,128]{2,1,0:T(8,128)(2,1)S(1)}, bf16[64,128]{1,0:T(8,128)(2,1)S(1)}, bf16[64,128]{1,0:T(8,128)(2,1)S(1)}, bf16[2,4,128,128]{3,2,1,0:T(8,128)(2,1)S(1)}) custom-call(bf16[64,128,128]{2,1,0:T(8,128)(2,1)} %q_hbm.1, bf16[64,128,128]{2,1,0:T(8,128)(2,1)} %g_hbm.1, bf16[64,128]{1,0:T(8,128)(2,1)} %lse_hbm.1, ...), custom_call_target="tpu_custom_call" | custom-call | flops 1 | bytes 1048576 | tf_op jit(solution)/shard_map/load/pallas_call | solution.py:209
  10.0 1.9 %collective-permute-start.3 = (bf16[2,4,128,128]{3,2,1,0:T(8,128)(2,1)S(1)}, bf16[2,4,128,128]{3,2,1,0:T(8,128)(2,1)S(1)}, u32[]{:S(2)}, u32[]{:S(2)}) collective-permute-start(bf16[2,4,128,128]{3,2,1,0:T(8,128)(2,1)S(1)} %get-tuple-element.33), channel_id=1, source_target_pairs={{0,128},{2,130},{4,132},{6,134},{8,136},{10,138},{12,140},{14,142}... | collective-permute-start | bytes 786440 | tf_op jit(solution)/shard_map/ppermute | solution.py:37
  12.0 0.0 collective-permute-done.refs_0_
  12.0 4.9 %collective-permute-start.2 = (bf16[2,4,128,128]{3,2,1,0:T(8,128)(2,1)S(1)}, bf16[2,4,128,128]{3,2,1,0:T(8,128)(2,1)S(1)}, u32[]{:S(2)}, u32[]{:S(2)}) collective-permute-start(bf16[2,4,128,128]{3,2,1,0:T(8,128)(2,1)S(1)} %collective-permute-done.refs_0_), channel_id=1, source_target_pairs={{0,129},{2,131},{4,133},{6,135},{8,137},{10,139},{12,141},{14,143}... | collective-permute-start | bytes 786440 | tf_op jit(solution)/shard_map/ppermute | solution.py:37
  16.8 1.3 %collective-permute-start.4 = (bf16[2,4,128,128]{3,2,1,0:T(8,128)(2,1)S(1)}, bf16[2,4,128,128]{3,2,1,0:T(8,128)(2,1)S(1)}, u32[]{:S(2)}, u32[]{:S(2)}) collective-permute-start(bf16[2,4,128,128]{3,2,1,0:T(8,128)(2,1)S(1)} %get-tuple-element.33), channel_id=1, source_target_pairs={{0,129},{2,131},{4,133},{6,135},{8,137},{10,139},{12,141},{14,143}... | collective-permute-start | bytes 786440 | tf_op jit(solution)/shard_map/ppermute | solution.py:37
  18.1 0.0 collective-permute-done.1.refs_1_
  18.2 1.3 %collective-permute-start.5 = (bf16[2,4,128,128]{3,2,1,0:T(8,128)(2,1)S(1)}, bf16[2,4,128,128]{3,2,1,0:T(8,128)(2,1)S(1)}, u32[]{:S(2)}, u32[]{:S(2)}) collective-permute-start(bf16[2,4,128,128]{3,2,1,0:T(8,128)(2,1)S(1)} %get-tuple-element.36), channel_id=1, source_target_pairs={{128,0},{130,2},{132,4},{134,6},{136,8},{138,10},{140,12},{142,14}... | collective-permute-start | bytes 786440 | tf_op jit(solution)/shard_map/ppermute | solution.py:37
  19.5 1.3 %collective-permute-start.6 = (bf16[2,4,128,128]{3,2,1,0:T(8,128)(2,1)S(1)}, bf16[2,4,128,128]{3,2,1,0:T(8,128)(2,1)S(1)}, u32[]{:S(2)}, u32[]{:S(2)}) collective-permute-start(bf16[2,4,128,128]{3,2,1,0:T(8,128)(2,1)S(1)} %get-tuple-element.37), channel_id=1, source_target_pairs={{129,0},{131,2},{133,4},{135,6},{137,8},{139,10},{141,12},{143,14}... | collective-permute-start | bytes 786440 | tf_op jit(solution)/shard_map/ppermute | solution.py:37
  20.8 0.0 collective-permute-done.3.refs_2_.refs_1_
  20.8 2.8 %collective-permute-done.2.refs_1_ = bf16[2,4,128,128]{3,2,1,0:T(8,128)(2,1)S(1)} collective-permute-done((bf16[2,4,128,128]{3,2,1,0:T(8,128)(2,1)S(1)}, bf16[2,4,128,128]{3,2,1,0:T(8,128)(2,1)S(1)}, u32[]{:S(2)}, u32[]{:S(2)}) %collective-permute-start.2) | collective-permute-done | bytes 262176 | tf_op jit(solution)/shard_map/ppermute | solution.py:37
  23.6 1.3 %collective-permute-start.7 = (bf16[2,4,128,128]{3,2,1,0:T(8,128)(2,1)S(1)}, bf16[2,4,128,128]{3,2,1,0:T(8,128)(2,1)S(1)}, u32[]{:S(2)}, u32[]{:S(2)}) collective-permute-start(bf16[2,4,128,128]{3,2,1,0:T(8,128)(2,1)S(1)} %get-tuple-element.38), channel_id=1, source_target_pairs={{1,0},{3,2},{5,4},{7,6},{9,8},{11,10},{13,12},{15,14},{17,16},{19,... | collective-permute-start | bytes 786440 | tf_op jit(solution)/shard_map/ppermute | solution.py:37
  24.9 7.3 %collective-permute-start.8 = (bf16[2,4,128,128]{3,2,1,0:T(8,128)(2,1)S(1)}, bf16[2,4,128,128]{3,2,1,0:T(8,128)(2,1)S(1)}, u32[]{:S(2)}, u32[]{:S(2)}) collective-permute-start(bf16[2,4,128,128]{3,2,1,0:T(8,128)(2,1)S(1)} %get-tuple-element.39), channel_id=1, source_target_pairs={{0,129},{2,131},{4,133},{6,135},{8,137},{10,139},{12,141},{14,143}... | collective-permute-start | bytes 786440 | tf_op jit(solution)/shard_map/ppermute | solution.py:37
  32.2 0.0 collective-permute-done.4.refs_2_
  32.2 1.3 %collective-permute-start.9 = (bf16[2,4,128,128]{3,2,1,0:T(8,128)(2,1)S(1)}, bf16[2,4,128,128]{3,2,1,0:T(8,128)(2,1)S(1)}, u32[]{:S(2)}, u32[]{:S(2)}) collective-permute-start(bf16[2,4,128,128]{3,2,1,0:T(8,128)(2,1)S(1)} %get-tuple-element.44), channel_id=1, source_target_pairs={{128,0},{130,2},{132,4},{134,6},{136,8},{138,10},{140,12},{142,14}... | collective-permute-start | bytes 786440 | tf_op jit(solution)/shard_map/ppermute | solution.py:37
  33.5 0.0 collective-permute-done.5.refs_1_
  33.5 1.3 %collective-permute-start.10 = (bf16[2,4,128,128]{3,2,1,0:T(8,128)(2,1)S(1)}, bf16[2,4,128,128]{3,2,1,0:T(8,128)(2,1)S(1)}, u32[]{:S(2)}, u32[]{:S(2)}) collective-permute-start(bf16[2,4,128,128]{3,2,1,0:T(8,128)(2,1)S(1)} %get-tuple-element.45), channel_id=1, source_target_pairs={{129,0},{131,2},{133,4},{135,6},{137,8},{139,10},{141,12},{143,14}... | collective-permute-start | bytes 786440 | tf_op jit(solution)/shard_map/ppermute | solution.py:37
  34.8 0.0 collective-permute-done.6.refs_2_
  34.8 0.0 collective-permute-done.7.refs_3_
  34.8 1.2 %collective-permute-done.8.refs_4_ = bf16[2,4,128,128]{3,2,1,0:T(8,128)(2,1)S(1)} collective-permute-done((bf16[2,4,128,128]{3,2,1,0:T(8,128)(2,1)S(1)}, bf16[2,4,128,128]{3,2,1,0:T(8,128)(2,1)S(1)}, u32[]{:S(2)}, u32[]{:S(2)}) %collective-permute-start.8) | collective-permute-done | bytes 262176 | tf_op jit(solution)/shard_map/ppermute | solution.py:37
  36.0 0.1 near1.1
  36.1 1.5 %collective-permute-start.11 = (bf16[2,4,128,128]{3,2,1,0:T(8,128)(2,1)S(1)}, bf16[2,4,128,128]{3,2,1,0:T(8,128)(2,1)S(1)}, u32[]{:S(2)}, u32[]{:S(2)}) collective-permute-start(bf16[2,4,128,128]{3,2,1,0:T(8,128)(2,1)S(1)} %get-tuple-element.46), channel_id=1, source_target_pairs={{1,0},{3,2},{5,4},{7,6},{9,8},{11,10},{13,12},{15,14},{17,16},{19,... | collective-permute-start | bytes 786440 | tf_op jit(solution)/shard_map/ppermute | solution.py:37
  37.6 4.0 %diag.1 = (bf16[64,128,128]{2,1,0:T(8,128)(2,1)}, f32[2,8,128,128]{3,2,1,0:T(8,128)S(1)}) custom-call(bf16[64,128,128]{2,1,0:T(8,128)(2,1)S(1)} %get-tuple-element.27.q_ref, bf16[64,128,128]{2,1,0:T(8,128)(2,1)S(1)} %get-tuple-element.28.g_ref, bf16[64,128]{1,0:T(8,128)(2,1)S(1)} %get-tuple-element.29.lse_ref, ...), custom_call_target="tpu_custom_call" | custom-call | flops 1 | bytes 1048576 | tf_op jit(solution)/shard_map/diag/pallas_call | solution.py:248
  41.6 0.0 collective-permute-done.9.rx_ref
  41.7 1.4 %collective-permute-done.10.ry_ref = bf16[2,4,128,128]{3,2,1,0:T(8,128)(2,1)S(1)} collective-permute-done((bf16[2,4,128,128]{3,2,1,0:T(8,128)(2,1)S(1)}, bf16[2,4,128,128]{3,2,1,0:T(8,128)(2,1)S(1)}, u32[]{:S(2)}, u32[]{:S(2)}) %collective-permute-start.10) | collective-permute-done | bytes 262176 | tf_op jit(solution)/shard_map/ppermute | solution.py:37
  43.1 3.5 %collective-permute-done.11.rz_ref = bf16[2,4,128,128]{3,2,1,0:T(8,128)(2,1)S(1)} collective-permute-done((bf16[2,4,128,128]{3,2,1,0:T(8,128)(2,1)S(1)}, bf16[2,4,128,128]{3,2,1,0:T(8,128)(2,1)S(1)}, u32[]{:S(2)}, u32[]{:S(2)}) %collective-permute-start.11) | collective-permute-done | bytes 262176 | tf_op jit(solution)/shard_map/ppermute | solution.py:37
  46.6 0.9 %final.1 = (bf16[8,128,128]{2,1,0:T(8,128)(2,1)}, bf16[8,128,128]{2,1,0:T(8,128)(2,1)}) custom-call(f32[2,8,128,128]{3,2,1,0:T(8,128)S(1)} %get-tuple-element.42.dkv_ref, f32[2,4,128,128]{3,2,1,0:T(8,128)S(1)} %get-tuple-element.43.sum_ref, bf16[2,4,128,128]{3,2,1,0:T(8,128)(2,1)S(1)} %collective-permute-done.9.rx_ref, ...), custom_call_target="tpu_custom_call" | custom-call | flops 1 | bytes 1048576 | tf_op jit(solution)/shard_map/final/pallas_call | solution.py:256
  (3 shorter events, 0.1 us)
Async XLA Ops:
  1.8 10.2 %collective-permute-start = (bf16[2,4,128,128]{3,2,1,0:T(8,128)(2,1)S(1)}, bf16[2,4,128,128]{3,2,1,0:T(8,128)(2,1)S(1)}, u32[]{:S(2)}, u32[]{:S(2)}) collective-permute-start(bf16[2,4,128,128]{3,2,1,0:T(8,128)(2,1)S(1)} %get-tuple-element.31.refs_0_), channel_id=1, source_target_pairs={{0,128},{2,130},{4,132},{6,134},{8,136},{10,138},{12,140},{14,142}... | collective-permute-start | bytes 786440 | tf_op jit(solution)/shard_map/ppermute | solution.py:37
  5.2 13.0 %collective-permute-start.1 = (bf16[2,4,128,128]{3,2,1,0:T(8,128)(2,1)S(1)}, bf16[2,4,128,128]{3,2,1,0:T(8,128)(2,1)S(1)}, u32[]{:S(2)}, u32[]{:S(2)}) collective-permute-start(bf16[2,4,128,128]{3,2,1,0:T(8,128)(2,1)S(1)} %get-tuple-element.31.refs_0_), channel_id=1, source_target_pairs={{0,129},{2,131},{4,133},{6,135},{8,137},{10,139},{12,141},{14,143}... | collective-permute-start | bytes 786440 | tf_op jit(solution)/shard_map/ppermute | solution.py:37
  10.0 10.8 %collective-permute-start.3 = (bf16[2,4,128,128]{3,2,1,0:T(8,128)(2,1)S(1)}, bf16[2,4,128,128]{3,2,1,0:T(8,128)(2,1)S(1)}, u32[]{:S(2)}, u32[]{:S(2)}) collective-permute-start(bf16[2,4,128,128]{3,2,1,0:T(8,128)(2,1)S(1)} %get-tuple-element.33), channel_id=1, source_target_pairs={{0,128},{2,130},{4,132},{6,134},{8,136},{10,138},{12,140},{14,142}... | collective-permute-start | bytes 786440 | tf_op jit(solution)/shard_map/ppermute | solution.py:37
  12.0 11.6 %collective-permute-start.2 = (bf16[2,4,128,128]{3,2,1,0:T(8,128)(2,1)S(1)}, bf16[2,4,128,128]{3,2,1,0:T(8,128)(2,1)S(1)}, u32[]{:S(2)}, u32[]{:S(2)}) collective-permute-start(bf16[2,4,128,128]{3,2,1,0:T(8,128)(2,1)S(1)} %collective-permute-done.refs_0_), channel_id=1, source_target_pairs={{0,129},{2,131},{4,133},{6,135},{8,137},{10,139},{12,141},{14,143}... | collective-permute-start | bytes 786440 | tf_op jit(solution)/shard_map/ppermute | solution.py:37
  16.8 15.3 %collective-permute-start.4 = (bf16[2,4,128,128]{3,2,1,0:T(8,128)(2,1)S(1)}, bf16[2,4,128,128]{3,2,1,0:T(8,128)(2,1)S(1)}, u32[]{:S(2)}, u32[]{:S(2)}) collective-permute-start(bf16[2,4,128,128]{3,2,1,0:T(8,128)(2,1)S(1)} %get-tuple-element.33), channel_id=1, source_target_pairs={{0,129},{2,131},{4,133},{6,135},{8,137},{10,139},{12,141},{14,143}... | collective-permute-start | bytes 786440 | tf_op jit(solution)/shard_map/ppermute | solution.py:37
  18.2 15.3 %collective-permute-start.5 = (bf16[2,4,128,128]{3,2,1,0:T(8,128)(2,1)S(1)}, bf16[2,4,128,128]{3,2,1,0:T(8,128)(2,1)S(1)}, u32[]{:S(2)}, u32[]{:S(2)}) collective-permute-start(bf16[2,4,128,128]{3,2,1,0:T(8,128)(2,1)S(1)} %get-tuple-element.36), channel_id=1, source_target_pairs={{128,0},{130,2},{132,4},{134,6},{136,8},{138,10},{140,12},{142,14}... | collective-permute-start | bytes 786440 | tf_op jit(solution)/shard_map/ppermute | solution.py:37
  19.5 15.3 %collective-permute-start.6 = (bf16[2,4,128,128]{3,2,1,0:T(8,128)(2,1)S(1)}, bf16[2,4,128,128]{3,2,1,0:T(8,128)(2,1)S(1)}, u32[]{:S(2)}, u32[]{:S(2)}) collective-permute-start(bf16[2,4,128,128]{3,2,1,0:T(8,128)(2,1)S(1)} %get-tuple-element.37), channel_id=1, source_target_pairs={{129,0},{131,2},{133,4},{135,6},{137,8},{139,10},{141,12},{143,14}... | collective-permute-start | bytes 786440 | tf_op jit(solution)/shard_map/ppermute | solution.py:37
  23.6 11.3 %collective-permute-start.7 = (bf16[2,4,128,128]{3,2,1,0:T(8,128)(2,1)S(1)}, bf16[2,4,128,128]{3,2,1,0:T(8,128)(2,1)S(1)}, u32[]{:S(2)}, u32[]{:S(2)}) collective-permute-start(bf16[2,4,128,128]{3,2,1,0:T(8,128)(2,1)S(1)} %get-tuple-element.38), channel_id=1, source_target_pairs={{1,0},{3,2},{5,4},{7,6},{9,8},{11,10},{13,12},{15,14},{17,16},{19,... | collective-permute-start | bytes 786440 | tf_op jit(solution)/shard_map/ppermute | solution.py:37
  24.9 11.2 %collective-permute-start.8 = (bf16[2,4,128,128]{3,2,1,0:T(8,128)(2,1)S(1)}, bf16[2,4,128,128]{3,2,1,0:T(8,128)(2,1)S(1)}, u32[]{:S(2)}, u32[]{:S(2)}) collective-permute-start(bf16[2,4,128,128]{3,2,1,0:T(8,128)(2,1)S(1)} %get-tuple-element.39), channel_id=1, source_target_pairs={{0,129},{2,131},{4,133},{6,135},{8,137},{10,139},{12,141},{14,143}... | collective-permute-start | bytes 786440 | tf_op jit(solution)/shard_map/ppermute | solution.py:37
  32.2 9.4 %collective-permute-start.9 = (bf16[2,4,128,128]{3,2,1,0:T(8,128)(2,1)S(1)}, bf16[2,4,128,128]{3,2,1,0:T(8,128)(2,1)S(1)}, u32[]{:S(2)}, u32[]{:S(2)}) collective-permute-start(bf16[2,4,128,128]{3,2,1,0:T(8,128)(2,1)S(1)} %get-tuple-element.44), channel_id=1, source_target_pairs={{128,0},{130,2},{132,4},{134,6},{136,8},{138,10},{140,12},{142,14}... | collective-permute-start | bytes 786440 | tf_op jit(solution)/shard_map/ppermute | solution.py:37
  33.5 9.5 %collective-permute-start.10 = (bf16[2,4,128,128]{3,2,1,0:T(8,128)(2,1)S(1)}, bf16[2,4,128,128]{3,2,1,0:T(8,128)(2,1)S(1)}, u32[]{:S(2)}, u32[]{:S(2)}) collective-permute-start(bf16[2,4,128,128]{3,2,1,0:T(8,128)(2,1)S(1)} %get-tuple-element.45), channel_id=1, source_target_pairs={{129,0},{131,2},{133,4},{135,6},{137,8},{139,10},{141,12},{143,14}... | collective-permute-start | bytes 786440 | tf_op jit(solution)/shard_map/ppermute | solution.py:37
  36.1 10.4 %collective-permute-start.11 = (bf16[2,4,128,128]{3,2,1,0:T(8,128)(2,1)S(1)}, bf16[2,4,128,128]{3,2,1,0:T(8,128)(2,1)S(1)}, u32[]{:S(2)}, u32[]{:S(2)}) collective-permute-start(bf16[2,4,128,128]{3,2,1,0:T(8,128)(2,1)S(1)} %get-tuple-element.46), channel_id=1, source_target_pairs={{1,0},{3,2},{5,4},{7,6},{9,8},{11,10},{13,12},{15,14},{17,16},{19,... | collective-permute-start | bytes 786440 | tf_op jit(solution)/shard_map/ppermute | solution.py:37

commit v4 on v3

--- a/solution.py
+++ b/solution.py
@@ -79,7 +79,7 @@
 
 
 def pack_kernel(k_ref, v_ref, *refs):
-    outs, sem = refs[:-1], refs[-1]
+    sources, outs, rows_refs, sem, rows_sem = refs[:4], refs[4:-6], refs[-6:-2], refs[-2], refs[-1]
     copies = []
     for i, out in enumerate(outs):
         n = out.shape[1]
@@ -87,6 +87,11 @@
             copies.append(pltpu.make_async_copy(src.at[pl.ds(i * n, n)], out.at[j], sem.at[2 * i + j]))
     for c in copies:
         c.start()
+
+    @pl.when(loads_first())
+    def _():
+        load_rows(sources, rows_refs, rows_sem)
+
     for c in copies:
         c.wait()
 
@@ -96,11 +101,8 @@
         out[...] = src[...]
 
 
-def load_kernel(q_hbm, g_hbm, lse_hbm, delta_hbm, *refs):
-    n = (len(refs) - 5) // 2
-    held, (q_ref, g_ref, lse_ref, delta_ref), later, sem = (
-        refs[:n], refs[n : n + 4], refs[n + 4 : -1], refs[-1]
-    )
+def load_rows(sources, targets, sem):
+    (q_hbm, g_hbm, lse_hbm, delta_hbm), (q_ref, g_ref, lse_ref, delta_ref) = sources, targets
     copies = [
         pltpu.make_async_copy(lse_hbm, lse_ref, sem.at[0]),
         pltpu.make_async_copy(delta_hbm, delta_ref, sem.at[1]),
@@ -113,9 +115,17 @@
         copies.append(pltpu.make_async_copy(g_hbm.at[cut], g_ref.at[cut], sem.at[3 + 2 * i]))
     for c in copies:
         c.start()
-    repeat(held, later)
-    for c in copies:
-        c.wait()
+    for c in copies:
+        c.wait()
+
+
+def load_kernel(*refs):
+    sources, held, rows_refs, later, sem = refs[:4], refs[8], refs[9:13], refs[13], refs[14]
+    later[...] = held[...]
+
+    @pl.when(jnp.logical_not(loads_first()))
+    def _():
+        load_rows(sources, rows_refs, sem)
 
 
 def pair_kernel(first, flag_at, n_kv, n_held, n_after, with_sum, q_ref, g_ref, lse_ref, delta_ref, *refs):
@@ -189,6 +199,10 @@
     return lax.axis_index("ctx") >= lax.axis_size("ctx") // 2
 
 
+def loads_first():
+    return lax.rem(lax.axis_index("ctx"), 2) == 0
+
+
 def in_hbm(x):
     return pltpu.with_memory_space_constraint(x, pltpu.HBM)
 
@@ -201,19 +215,27 @@
     part = shape((2, n, rows, width), BF16)
     dq_part = shape((heads // CHUNKS, rows, width), F32)
     sem = pltpu.SemaphoreType.DMA
-    parts = call(
-        pack_kernel, "pack", [HBM] * 2, [VMEM] * CHUNKS, [part] * CHUNKS, [sem((2 * CHUNKS,))]
-    )(in_hbm(keys), in_hbm(values))
+    rows_hbm = [in_hbm(x) for x in (queries, grad_out, lse, delta)]
+    rows_shape = [shape(x.shape, BF16) for x in rows_hbm]
+    *parts, r0, r1, r2, r3 = call(
+        pack_kernel,
+        "pack",
+        [HBM] * 6,
+        [VMEM] * (CHUNKS + 4),
+        [part] * CHUNKS + rows_shape,
+        [sem((2 * CHUNKS,)), sem((10,))],
+    )(in_hbm(keys), in_hbm(values), *rows_hbm)
 
     up0, down0 = route(parts[0], "E0>L0 E1>L1 L0>E0"), route(parts[0], "E0>L1 E1>L0")
     *rows_in, later = call(
         load_kernel,
         "load",
-        [HBM] * 4 + [VMEM],
+        [HBM] * 4 + [VMEM] * 5,
         [VMEM] * 5,
-        [shape(x.shape, BF16) for x in (queries, grad_out, lse, delta)] + [part],
+        rows_shape + [part],
         [sem((10,))],
-    )(*(in_hbm(x) for x in (queries, grad_out, lse, delta)), parts[1])
+        {4: 0, 5: 1, 6: 2, 7: 3},
+    )(*rows_hbm, r0, r1, r2, r3, parts[1])
     up1, down1 = route(later, "E0>L0 E1>L1 L0>E0"), route(later, "E0>L1 E1>L0")
 
     def to_second(x):

time: 48.1 us -> 47.4 us (0.985)
  Pallas kernels: 8.46 us -> 7.72 us
    pallas_call x2, Pallas kernels: 3.4 us -> 2.66 us  [the longest x1 2.54 us: local(): call(pack_kernel, 'pack', [HBM] * 6, [VMEM] * (CHUNKS + 4), [part] * CHUN...]
  transfers between devices with their start and end apart: 12 -> 12, of which waited for: 4 -> 5; matrix products, arithmetic and copies ran while one was open for 0% -> 0% of each run, Pallas kernels for 14% -> 9%
where the time goes in v4:
time: 47.4 us; the launch traced here: 47 us
  starting transfers between devices  29.5 us (62%)
  waiting for transfers between devices  8.77 us (19%)
  Pallas kernels  7.72 us (16%)
  between operations  0.98 us (2%)
    ppermute x12, starting transfers between devices, route(): return lax.ppermute(x, AXES, table)  29.5 us
    ppermute x12, waiting for transfers between devices, route(): return lax.ppermute(x, AXES, table)  8.77 us
    pallas_call x1, Pallas kernels, local(): call(diag_kernel, 'diag', [VMEM] * 10, [HBM, VMEM], [shape(queries.shape,...  4.03 us
    pallas_call x1, Pallas kernels, local(): call(pack_kernel, 'pack', [HBM] * 6, [VMEM] * (CHUNKS + 4), [part] * CHUN...  2.54 us
  transfers between devices with their start and end apart: 12, of which 5 were waited for; matrix products, arithmetic and copies ran while one was open for 0% of the time, Pallas kernels for 9%

profile of v4, /device:TPU:72, one launch (start us, length us, event | category | flops | bytes accessed | tf_op | source)
XLA Modules:
  0.0 47.0 jit_solution(6970349413173837600)
XLA Ops:
  0.6 2.5 %pack.1 = (bf16[2,4,128,128]{3,2,1,0:T(8,128)(2,1)S(1)}, bf16[2,4,128,128]{3,2,1,0:T(8,128)(2,1)S(1)}, bf16[64,128,128]{2,1,0:T(8,128)(2,1)S(1)}, bf16[64,128,12...) custom-call(bf16[8,128,128]{2,1,0:T(8,128)(2,1)} %k_ref.1, ...), custom_call_target="tpu_custom_call" | custom-call | flops 1 | bytes 1048576 | tf_op jit(solution)/shard_map/pack/pallas_call | solution.py:220
  3.2 3.4 %collective-permute-start = (bf16[2,4,128,128]{3,2,1,0:T(8,128)(2,1)S(1)}, bf16[2,4,128,128]{3,2,1,0:T(8,128)(2,1)S(1)}, u32[]{:S(2)}, u32[]{:S(2)}) collective-permute-start(bf16[2,4,128,128]{3,2,1,0:T(8,128)(2,1)S(1)} %get-tuple-element.39.refs_0_), channel_id=1, source_target_pairs={{0,128},{2,130},{4,132},{6,134},{8,136},{10,138},{12,140},{14,142}... | collective-permute-start | bytes 786440 | tf_op jit(solution)/shard_map/ppermute | solution.py:37
  6.6 2.6 %collective-permute-start.1 = (bf16[2,4,128,128]{3,2,1,0:T(8,128)(2,1)S(1)}, bf16[2,4,128,128]{3,2,1,0:T(8,128)(2,1)S(1)}, u32[]{:S(2)}, u32[]{:S(2)}) collective-permute-start(bf16[2,4,128,128]{3,2,1,0:T(8,128)(2,1)S(1)} %get-tuple-element.39.refs_0_), channel_id=1, source_target_pairs={{0,129},{2,131},{4,133},{6,135},{8,137},{10,139},{12,141},{14,143}... | collective-permute-start | bytes 786440 | tf_op jit(solution)/shard_map/ppermute | solution.py:37
  9.2 0.1 load.1
  9.3 1.9 %collective-permute-start.3 = (bf16[2,4,128,128]{3,2,1,0:T(8,128)(2,1)S(1)}, bf16[2,4,128,128]{3,2,1,0:T(8,128)(2,1)S(1)}, u32[]{:S(2)}, u32[]{:S(2)}) collective-permute-start(bf16[2,4,128,128]{3,2,1,0:T(8,128)(2,1)S(1)} %get-tuple-element.41), channel_id=1, source_target_pairs={{0,128},{2,130},{4,132},{6,134},{8,136},{10,138},{12,140},{14,142}... | collective-permute-start | bytes 786440 | tf_op jit(solution)/shard_map/ppermute | solution.py:37
  11.2 0.6 %collective-permute-done.refs_0_ = bf16[2,4,128,128]{3,2,1,0:T(8,128)(2,1)S(1)} collective-permute-done((bf16[2,4,128,128]{3,2,1,0:T(8,128)(2,1)S(1)}, bf16[2,4,128,128]{3,2,1,0:T(8,128)(2,1)S(1)}, u32[]{:S(2)}, u32[]{:S(2)}) %collective-permute-start) | collective-permute-done | bytes 262176 | tf_op jit(solution)/shard_map/ppermute | solution.py:37
  11.8 5.1 %collective-permute-start.2 = (bf16[2,4,128,128]{3,2,1,0:T(8,128)(2,1)S(1)}, bf16[2,4,128,128]{3,2,1,0:T(8,128)(2,1)S(1)}, u32[]{:S(2)}, u32[]{:S(2)}) collective-permute-start(bf16[2,4,128,128]{3,2,1,0:T(8,128)(2,1)S(1)} %collective-permute-done.refs_0_), channel_id=1, source_target_pairs={{0,129},{2,131},{4,133},{6,135},{8,137},{10,139},{12,141},{14,143}... | collective-permute-start | bytes 786440 | tf_op jit(solution)/shard_map/ppermute | solution.py:37
  16.9 1.3 %collective-permute-start.4 = (bf16[2,4,128,128]{3,2,1,0:T(8,128)(2,1)S(1)}, bf16[2,4,128,128]{3,2,1,0:T(8,128)(2,1)S(1)}, u32[]{:S(2)}, u32[]{:S(2)}) collective-permute-start(bf16[2,4,128,128]{3,2,1,0:T(8,128)(2,1)S(1)} %get-tuple-element.41), channel_id=1, source_target_pairs={{0,129},{2,131},{4,133},{6,135},{8,137},{10,139},{12,141},{14,143}... | collective-permute-start | bytes 786440 | tf_op jit(solution)/shard_map/ppermute | solution.py:37
  18.2 0.0 collective-permute-done.1.refs_1_
  18.3 1.3 %collective-permute-start.5 = (bf16[2,4,128,128]{3,2,1,0:T(8,128)(2,1)S(1)}, bf16[2,4,128,128]{3,2,1,0:T(8,128)(2,1)S(1)}, u32[]{:S(2)}, u32[]{:S(2)}) collective-permute-start(bf16[2,4,128,128]{3,2,1,0:T(8,128)(2,1)S(1)} %get-tuple-element.44), channel_id=1, source_target_pairs={{128,0},{130,2},{132,4},{134,6},{136,8},{138,10},{140,12},{142,14}... | collective-permute-start | bytes 786440 | tf_op jit(solution)/shard_map/ppermute | solution.py:37
  19.6 1.3 %collective-permute-start.6 = (bf16[2,4,128,128]{3,2,1,0:T(8,128)(2,1)S(1)}, bf16[2,4,128,128]{3,2,1,0:T(8,128)(2,1)S(1)}, u32[]{:S(2)}, u32[]{:S(2)}) collective-permute-start(bf16[2,4,128,128]{3,2,1,0:T(8,128)(2,1)S(1)} %get-tuple-element.45), channel_id=1, source_target_pairs={{129,0},{131,2},{133,4},{135,6},{137,8},{139,10},{141,12},{143,14}... | collective-permute-start | bytes 786440 | tf_op jit(solution)/shard_map/ppermute | solution.py:37
  20.9 0.0 collective-permute-done.3.refs_2_.refs_1_
  20.9 1.7 %collective-permute-done.2.refs_1_ = bf16[2,4,128,128]{3,2,1,0:T(8,128)(2,1)S(1)} collective-permute-done((bf16[2,4,128,128]{3,2,1,0:T(8,128)(2,1)S(1)}, bf16[2,4,128,128]{3,2,1,0:T(8,128)(2,1)S(1)}, u32[]{:S(2)}, u32[]{:S(2)}) %collective-permute-start.2) | collective-permute-done | bytes 262176 | tf_op jit(solution)/shard_map/ppermute | solution.py:37
  22.6 1.3 %collective-permute-start.7 = (bf16[2,4,128,128]{3,2,1,0:T(8,128)(2,1)S(1)}, bf16[2,4,128,128]{3,2,1,0:T(8,128)(2,1)S(1)}, u32[]{:S(2)}, u32[]{:S(2)}) collective-permute-start(bf16[2,4,128,128]{3,2,1,0:T(8,128)(2,1)S(1)} %get-tuple-element.46), channel_id=1, source_target_pairs={{1,0},{3,2},{5,4},{7,6},{9,8},{11,10},{13,12},{15,14},{17,16},{19,... | collective-permute-start | bytes 786440 | tf_op jit(solution)/shard_map/ppermute | solution.py:37
  23.9 7.3 %collective-permute-start.8 = (bf16[2,4,128,128]{3,2,1,0:T(8,128)(2,1)S(1)}, bf16[2,4,128,128]{3,2,1,0:T(8,128)(2,1)S(1)}, u32[]{:S(2)}, u32[]{:S(2)}) collective-permute-start(bf16[2,4,128,128]{3,2,1,0:T(8,128)(2,1)S(1)} %get-tuple-element.47), channel_id=1, source_target_pairs={{0,129},{2,131},{4,133},{6,135},{8,137},{10,139},{12,141},{14,143}... | collective-permute-start | bytes 786440 | tf_op jit(solution)/shard_map/ppermute | solution.py:37
  31.2 0.0 collective-permute-done.4.refs_2_
  31.3 1.3 %collective-permute-start.9 = (bf16[2,4,128,128]{3,2,1,0:T(8,128)(2,1)S(1)}, bf16[2,4,128,128]{3,2,1,0:T(8,128)(2,1)S(1)}, u32[]{:S(2)}, u32[]{:S(2)}) collective-permute-start(bf16[2,4,128,128]{3,2,1,0:T(8,128)(2,1)S(1)} %get-tuple-element.52), channel_id=1, source_target_pairs={{128,0},{130,2},{132,4},{134,6},{136,8},{138,10},{140,12},{142,14}... | collective-permute-start | bytes 786440 | tf_op jit(solution)/shard_map/ppermute | solution.py:37
  32.6 0.0 collective-permute-done.5.refs_1_
  32.6 1.3 %collective-permute-start.10 = (bf16[2,4,128,128]{3,2,1,0:T(8,128)(2,1)S(1)}, bf16[2,4,128,128]{3,2,1,0:T(8,128)(2,1)S(1)}, u32[]{:S(2)}, u32[]{:S(2)}) collective-permute-start(bf16[2,4,128,128]{3,2,1,0:T(8,128)(2,1)S(1)} %get-tuple-element.53), channel_id=1, source_target_pairs={{129,0},{131,2},{133,4},{135,6},{137,8},{139,10},{141,12},{143,14}... | collective-permute-start | bytes 786440 | tf_op jit(solution)/shard_map/ppermute | solution.py:37
  33.9 0.2 collective-permute-done.6.refs_2_
  34.0 0.0 collective-permute-done.7.refs_3_
  34.0 1.0 %collective-permute-done.8.refs_4_ = bf16[2,4,128,128]{3,2,1,0:T(8,128)(2,1)S(1)} collective-permute-done((bf16[2,4,128,128]{3,2,1,0:T(8,128)(2,1)S(1)}, bf16[2,4,128,128]{3,2,1,0:T(8,128)(2,1)S(1)}, u32[]{:S(2)}, u32[]{:S(2)}) %collective-permute-start.8) | collective-permute-done | bytes 262176 | tf_op jit(solution)/shard_map/ppermute | solution.py:37
  35.1 0.1 near1.1
  35.2 1.5 %collective-permute-start.11 = (bf16[2,4,128,128]{3,2,1,0:T(8,128)(2,1)S(1)}, bf16[2,4,128,128]{3,2,1,0:T(8,128)(2,1)S(1)}, u32[]{:S(2)}, u32[]{:S(2)}) collective-permute-start(bf16[2,4,128,128]{3,2,1,0:T(8,128)(2,1)S(1)} %get-tuple-element.54), channel_id=1, source_target_pairs={{1,0},{3,2},{5,4},{7,6},{9,8},{11,10},{13,12},{15,14},{17,16},{19,... | collective-permute-start | bytes 786440 | tf_op jit(solution)/shard_map/ppermute | solution.py:37
  36.6 4.0 %diag.1 = (bf16[64,128,128]{2,1,0:T(8,128)(2,1)}, f32[2,8,128,128]{3,2,1,0:T(8,128)S(1)}) custom-call(bf16[64,128,128]{2,1,0:T(8,128)(2,1)S(1)} %get-tuple-element.35.q_ref, bf16[64,128,128]{2,1,0:T(8,128)(2,1)S(1)} %get-tuple-element.36.g_ref, bf16[64,128]{1,0:T(8,128)(2,1)S(1)} %get-tuple-element.37.lse_ref, ...), custom_call_target="tpu_custom_call" | custom-call | flops 1 | bytes 1048576 | tf_op jit(solution)/shard_map/diag/pallas_call | solution.py:270
  40.7 0.0 collective-permute-done.9.rx_ref
  40.7 5.2 %collective-permute-done.10.ry_ref = bf16[2,4,128,128]{3,2,1,0:T(8,128)(2,1)S(1)} collective-permute-done((bf16[2,4,128,128]{3,2,1,0:T(8,128)(2,1)S(1)}, bf16[2,4,128,128]{3,2,1,0:T(8,128)(2,1)S(1)}, u32[]{:S(2)}, u32[]{:S(2)}) %collective-permute-start.10) | collective-permute-done | bytes 262176 | tf_op jit(solution)/shard_map/ppermute | solution.py:37
  45.9 0.0 collective-permute-done.11.rz_ref
  45.9 0.9 %final.1 = (bf16[8,128,128]{2,1,0:T(8,128)(2,1)}, bf16[8,128,128]{2,1,0:T(8,128)(2,1)}) custom-call(f32[2,8,128,128]{3,2,1,0:T(8,128)S(1)} %get-tuple-element.50.dkv_ref, f32[2,4,128,128]{3,2,1,0:T(8,128)S(1)} %get-tuple-element.51.sum_ref, bf16[2,4,128,128]{3,2,1,0:T(8,128)(2,1)S(1)} %collective-permute-done.9.rx_ref, ...), custom_call_target="tpu_custom_call" | custom-call | flops 1 | bytes 1048576 | tf_op jit(solution)/shard_map/final/pallas_call | solution.py:278
  (3 shorter events, 0.1 us)
Async XLA Ops:
  3.2 8.6 %collective-permute-start = (bf16[2,4,128,128]{3,2,1,0:T(8,128)(2,1)S(1)}, bf16[2,4,128,128]{3,2,1,0:T(8,128)(2,1)S(1)}, u32[]{:S(2)}, u32[]{:S(2)}) collective-permute-start(bf16[2,4,128,128]{3,2,1,0:T(8,128)(2,1)S(1)} %get-tuple-element.39.refs_0_), channel_id=1, source_target_pairs={{0,128},{2,130},{4,132},{6,134},{8,136},{10,138},{12,140},{14,142}... | collective-permute-start | bytes 786440 | tf_op jit(solution)/shard_map/ppermute | solution.py:37
  6.6 11.7 %collective-permute-start.1 = (bf16[2,4,128,128]{3,2,1,0:T(8,128)(2,1)S(1)}, bf16[2,4,128,128]{3,2,1,0:T(8,128)(2,1)S(1)}, u32[]{:S(2)}, u32[]{:S(2)}) collective-permute-start(bf16[2,4,128,128]{3,2,1,0:T(8,128)(2,1)S(1)} %get-tuple-element.39.refs_0_), channel_id=1, source_target_pairs={{0,129},{2,131},{4,133},{6,135},{8,137},{10,139},{12,141},{14,143}... | collective-permute-start | bytes 786440 | tf_op jit(solution)/shard_map/ppermute | solution.py:37
  9.3 11.6 %collective-permute-start.3 = (bf16[2,4,128,128]{3,2,1,0:T(8,128)(2,1)S(1)}, bf16[2,4,128,128]{3,2,1,0:T(8,128)(2,1)S(1)}, u32[]{:S(2)}, u32[]{:S(2)}) collective-permute-start(bf16[2,4,128,128]{3,2,1,0:T(8,128)(2,1)S(1)} %get-tuple-element.41), channel_id=1, source_target_pairs={{0,128},{2,130},{4,132},{6,134},{8,136},{10,138},{12,140},{14,142}... | collective-permute-start | bytes 786440 | tf_op jit(solution)/shard_map/ppermute | solution.py:37
  11.8 10.8 %collective-permute-start.2 = (bf16[2,4,128,128]{3,2,1,0:T(8,128)(2,1)S(1)}, bf16[2,4,128,128]{3,2,1,0:T(8,128)(2,1)S(1)}, u32[]{:S(2)}, u32[]{:S(2)}) collective-permute-start(bf16[2,4,128,128]{3,2,1,0:T(8,128)(2,1)S(1)} %collective-permute-done.refs_0_), channel_id=1, source_target_pairs={{0,129},{2,131},{4,133},{6,135},{8,137},{10,139},{12,141},{14,143}... | collective-permute-start | bytes 786440 | tf_op jit(solution)/shard_map/ppermute | solution.py:37
  16.9 14.3 %collective-permute-start.4 = (bf16[2,4,128,128]{3,2,1,0:T(8,128)(2,1)S(1)}, bf16[2,4,128,128]{3,2,1,0:T(8,128)(2,1)S(1)}, u32[]{:S(2)}, u32[]{:S(2)}) collective-permute-start(bf16[2,4,128,128]{3,2,1,0:T(8,128)(2,1)S(1)} %get-tuple-element.41), channel_id=1, source_target_pairs={{0,129},{2,131},{4,133},{6,135},{8,137},{10,139},{12,141},{14,143}... | collective-permute-start | bytes 786440 | tf_op jit(solution)/shard_map/ppermute | solution.py:37
  18.3 14.3 %collective-permute-start.5 = (bf16[2,4,128,128]{3,2,1,0:T(8,128)(2,1)S(1)}, bf16[2,4,128,128]{3,2,1,0:T(8,128)(2,1)S(1)}, u32[]{:S(2)}, u32[]{:S(2)}) collective-permute-start(bf16[2,4,128,128]{3,2,1,0:T(8,128)(2,1)S(1)} %get-tuple-element.44), channel_id=1, source_target_pairs={{128,0},{130,2},{132,4},{134,6},{136,8},{138,10},{140,12},{142,14}... | collective-permute-start | bytes 786440 | tf_op jit(solution)/shard_map/ppermute | solution.py:37
  19.6 14.5 %collective-permute-start.6 = (bf16[2,4,128,128]{3,2,1,0:T(8,128)(2,1)S(1)}, bf16[2,4,128,128]{3,2,1,0:T(8,128)(2,1)S(1)}, u32[]{:S(2)}, u32[]{:S(2)}) collective-permute-start(bf16[2,4,128,128]{3,2,1,0:T(8,128)(2,1)S(1)} %get-tuple-element.45), channel_id=1, source_target_pairs={{129,0},{131,2},{133,4},{135,6},{137,8},{139,10},{141,12},{143,14}... | collective-permute-start | bytes 786440 | tf_op jit(solution)/shard_map/ppermute | solution.py:37
  22.6 11.4 %collective-permute-start.7 = (bf16[2,4,128,128]{3,2,1,0:T(8,128)(2,1)S(1)}, bf16[2,4,128,128]{3,2,1,0:T(8,128)(2,1)S(1)}, u32[]{:S(2)}, u32[]{:S(2)}) collective-permute-start(bf16[2,4,128,128]{3,2,1,0:T(8,128)(2,1)S(1)} %get-tuple-element.46), channel_id=1, source_target_pairs={{1,0},{3,2},{5,4},{7,6},{9,8},{11,10},{13,12},{15,14},{17,16},{19,... | collective-permute-start | bytes 786440 | tf_op jit(solution)/shard_map/ppermute | solution.py:37
  23.9 11.2 %collective-permute-start.8 = (bf16[2,4,128,128]{3,2,1,0:T(8,128)(2,1)S(1)}, bf16[2,4,128,128]{3,2,1,0:T(8,128)(2,1)S(1)}, u32[]{:S(2)}, u32[]{:S(2)}) collective-permute-start(bf16[2,4,128,128]{3,2,1,0:T(8,128)(2,1)S(1)} %get-tuple-element.47), channel_id=1, source_target_pairs={{0,129},{2,131},{4,133},{6,135},{8,137},{10,139},{12,141},{14,143}... | collective-permute-start | bytes 786440 | tf_op jit(solution)/shard_map/ppermute | solution.py:37
  31.3 9.4 %collective-permute-start.9 = (bf16[2,4,128,128]{3,2,1,0:T(8,128)(2,1)S(1)}, bf16[2,4,128,128]{3,2,1,0:T(8,128)(2,1)S(1)}, u32[]{:S(2)}, u32[]{:S(2)}) collective-permute-start(bf16[2,4,128,128]{3,2,1,0:T(8,128)(2,1)S(1)} %get-tuple-element.52), channel_id=1, source_target_pairs={{128,0},{130,2},{132,4},{134,6},{136,8},{138,10},{140,12},{142,14}... | collective-permute-start | bytes 786440 | tf_op jit(solution)/shard_map/ppermute | solution.py:37
  32.6 13.4 %collective-permute-start.10 = (bf16[2,4,128,128]{3,2,1,0:T(8,128)(2,1)S(1)}, bf16[2,4,128,128]{3,2,1,0:T(8,128)(2,1)S(1)}, u32[]{:S(2)}, u32[]{:S(2)}) collective-permute-start(bf16[2,4,128,128]{3,2,1,0:T(8,128)(2,1)S(1)} %get-tuple-element.53), channel_id=1, source_target_pairs={{129,0},{131,2},{133,4},{135,6},{137,8},{139,10},{141,12},{143,14}... | collective-permute-start | bytes 786440 | tf_op jit(solution)/shard_map/ppermute | solution.py:37
  35.2 10.8 %collective-permute-start.11 = (bf16[2,4,128,128]{3,2,1,0:T(8,128)(2,1)S(1)}, bf16[2,4,128,128]{3,2,1,0:T(8,128)(2,1)S(1)}, u32[]{:S(2)}, u32[]{:S(2)}) collective-permute-start(bf16[2,4,128,128]{3,2,1,0:T(8,128)(2,1)S(1)} %get-tuple-element.54), channel_id=1, source_target_pairs={{1,0},{3,2},{5,4},{7,6},{9,8},{11,10},{13,12},{15,14},{17,16},{19,... | collective-permute-start | bytes 786440 | tf_op jit(solution)/shard_map/ppermute | solution.py:37

commit v5 on v4

--- a/solution.py
+++ b/solution.py
@@ -156,7 +156,7 @@
 
 def diag_kernel(q_ref, g_ref, lse_ref, delta_ref, *refs):
     parts, near_refs, far_refs = refs[0:2], refs[2:4], refs[4:6]
-    dq_hbm, dkv_ref, dq_half, sem = refs[6:]
+    far_sum, dq_hbm, dk_hbm, dv_hbm, dkv_ref, dq_half, half, sem, kv_sem = refs[6:]
     n = parts[0].shape[1]
     ratio = 8
     stores = []
@@ -172,20 +172,30 @@
         cut = pl.ds(g * ratio, ratio)
         stores.append(pltpu.make_async_copy(dq_half.at[cut], dq_hbm.at[cut], sem.at[g]))
         stores[-1].start()
-        dkv_ref[0, g] = dk
-        dkv_ref[1, g] = dv
+        if c:
+            dkv_ref[0, i] = dk
+            dkv_ref[1, i] = dv
+        else:
+            half[0, i] = (dk + far_sum[0, i]).astype(BF16)
+            half[1, i] = (dv + far_sum[1, i]).astype(BF16)
+        if g == n - 1:
+            for j, out in enumerate((dk_hbm, dv_hbm)):
+                stores.append(
+                    pltpu.make_async_copy(half.at[j], out.at[pl.ds(0, n)], kv_sem.at[j])
+                )
+                stores[-1].start()
     for c in stores:
         c.wait()
 
 
-def final_kernel(dkv_ref, sum_ref, rx_ref, ry_ref, rz_ref, dk_hbm, dv_hbm, half, sem):
+def final_kernel(dkv_ref, rx_ref, ry_ref, rz_ref, *refs):
+    dk_hbm, dv_hbm, half, sem = refs[-4:]
     n = rz_ref.shape[1]
     copies = []
     for j, out in enumerate((dk_hbm, dv_hbm)):
-        half[j, :n] = (dkv_ref[j, :n] + sum_ref[j]).astype(BF16)
         far = rx_ref[j].astype(F32) + ry_ref[j].astype(F32)
-        half[j, n:] = (dkv_ref[j, n:] + rz_ref[j].astype(F32) + far).astype(BF16)
-        copies.append(pltpu.make_async_copy(half.at[j], out, sem.at[j]))
+        half[j] = (dkv_ref[j] + rz_ref[j].astype(F32) + far).astype(BF16)
+        copies.append(pltpu.make_async_copy(half.at[j], out.at[pl.ds(n, n)], sem.at[j]))
         copies[-1].start()
     for c in copies:
         c.wait()
@@ -266,23 +276,29 @@
     rx1, ry1 = to_early(dx1, dy1)
     dq_near1, dz1, far_sum = pairs("near1", 0, [kv_near1], add=[rx0, ry0, rz0], after=[dq_far1])
     rz1 = route(dz1, "E1>E0 L1>L0")
-    whole = (2, groups, rows, width)
-    dq, dkv = call(
+    whole = shape(keys.shape, BF16)
+    dq, dk, dv, dkv = call(
         diag_kernel,
         "diag",
-        [VMEM] * 10,
-        [HBM, VMEM],
-        [shape(queries.shape, BF16), shape(whole, F32)],
-        [pltpu.VMEM(queries.shape, BF16), sem((groups,))],
-    )(*rows_in, *parts, dq_near0, dq_near1, dq_far0, dq_far1)
+        [VMEM] * 11,
+        [HBM] * 3 + [VMEM],
+        [shape(queries.shape, BF16), whole, whole, shape(part.shape, F32)],
+        [
+            pltpu.VMEM(queries.shape, BF16),
+            pltpu.VMEM(part.shape, BF16),
+            sem((groups,)),
+            sem((2,)),
+        ],
+    )(*rows_in, *parts, dq_near0, dq_near1, dq_far0, dq_far1, far_sum)
     dk, dv = call(
         final_kernel,
         "final",
-        [VMEM] * 5,
+        [VMEM] * 4 + [HBM] * 2,
         [HBM] * 2,
-        [shape(keys.shape, BF16)] * 2,
-        [pltpu.VMEM(whole, BF16), sem((2,))],
-    )(dkv, far_sum, rx1, ry1, rz1)
+        [whole] * 2,
+        [pltpu.VMEM(part.shape, BF16), sem((2,))],
+        {4: 0, 5: 1},
+    )(dkv, rx1, ry1, rz1, dk, dv)
     return dq, dk, dv
 
 

time: 47.4 us -> 47.3 us (level)
  transfers between devices with their start and end apart: 12 -> 12, of which waited for: 5 -> 5; matrix products, arithmetic and copies ran while one was open for 0% -> 0% of each run, Pallas kernels for 9% -> 10%
where the time goes in v5:
time: 47.3 us; the launch traced here: 46.9 us
  starting transfers between devices  29.5 us (62%)
  waiting for transfers between devices  8.54 us (18%)
  Pallas kernels  7.85 us (17%)
  between operations  0.98 us (2%)
    ppermute x12, starting transfers between devices, route(): return lax.ppermute(x, AXES, table)  29.5 us
    ppermute x12, waiting for transfers between devices, route(): return lax.ppermute(x, AXES, table)  8.54 us
    pallas_call x1, Pallas kernels, local(): call(diag_kernel, 'diag', [VMEM] * 11, [HBM] * 3 + [VMEM], [shape(queries...  4.25 us
    pallas_call x1, Pallas kernels, local(): call(pack_kernel, 'pack', [HBM] * 6, [VMEM] * (CHUNKS + 4), [part] * CHUN...  2.54 us
  transfers between devices with their start and end apart: 12, of which 5 were waited for; matrix products, arithmetic and copies ran while one was open for 0% of the time, Pallas kernels for 10%

profile of v5, /device:TPU:72, one launch (start us, length us, event | category | flops | bytes accessed | tf_op | source)
XLA Modules:
  0.0 46.9 jit_solution(3436401752385101253)
XLA Ops:
  0.6 2.5 %pack.1 = (bf16[2,4,128,128]{3,2,1,0:T(8,128)(2,1)S(1)}, bf16[2,4,128,128]{3,2,1,0:T(8,128)(2,1)S(1)}, bf16[64,128,128]{2,1,0:T(8,128)(2,1)S(1)}, bf16[64,128,12...) custom-call(bf16[8,128,128]{2,1,0:T(8,128)(2,1)} %k_ref.1, ...), custom_call_target="tpu_custom_call" | custom-call | flops 1 | bytes 1048576 | tf_op jit(solution)/shard_map/pack/pallas_call | solution.py:230
  3.2 3.4 %collective-permute-start = (bf16[2,4,128,128]{3,2,1,0:T(8,128)(2,1)S(1)}, bf16[2,4,128,128]{3,2,1,0:T(8,128)(2,1)S(1)}, u32[]{:S(2)}, u32[]{:S(2)}) collective-permute-start(bf16[2,4,128,128]{3,2,1,0:T(8,128)(2,1)S(1)} %get-tuple-element.41.refs_0_), channel_id=1, source_target_pairs={{0,128},{2,130},{4,132},{6,134},{8,136},{10,138},{12,140},{14,142}... | collective-permute-start | bytes 786440 | tf_op jit(solution)/shard_map/ppermute | solution.py:37
  6.6 2.6 %collective-permute-start.1 = (bf16[2,4,128,128]{3,2,1,0:T(8,128)(2,1)S(1)}, bf16[2,4,128,128]{3,2,1,0:T(8,128)(2,1)S(1)}, u32[]{:S(2)}, u32[]{:S(2)}) collective-permute-start(bf16[2,4,128,128]{3,2,1,0:T(8,128)(2,1)S(1)} %get-tuple-element.41.refs_0_), channel_id=1, source_target_pairs={{0,129},{2,131},{4,133},{6,135},{8,137},{10,139},{12,141},{14,143}... | collective-permute-start | bytes 786440 | tf_op jit(solution)/shard_map/ppermute | solution.py:37
  9.2 0.1 load.1
  9.3 1.9 %collective-permute-start.3 = (bf16[2,4,128,128]{3,2,1,0:T(8,128)(2,1)S(1)}, bf16[2,4,128,128]{3,2,1,0:T(8,128)(2,1)S(1)}, u32[]{:S(2)}, u32[]{:S(2)}) collective-permute-start(bf16[2,4,128,128]{3,2,1,0:T(8,128)(2,1)S(1)} %get-tuple-element.43), channel_id=1, source_target_pairs={{0,128},{2,130},{4,132},{6,134},{8,136},{10,138},{12,140},{14,142}... | collective-permute-start | bytes 786440 | tf_op jit(solution)/shard_map/ppermute | solution.py:37
  11.2 0.6 %collective-permute-done.refs_0_ = bf16[2,4,128,128]{3,2,1,0:T(8,128)(2,1)S(1)} collective-permute-done((bf16[2,4,128,128]{3,2,1,0:T(8,128)(2,1)S(1)}, bf16[2,4,128,128]{3,2,1,0:T(8,128)(2,1)S(1)}, u32[]{:S(2)}, u32[]{:S(2)}) %collective-permute-start) | collective-permute-done | bytes 262176 | tf_op jit(solution)/shard_map/ppermute | solution.py:37
  11.8 5.1 %collective-permute-start.2 = (bf16[2,4,128,128]{3,2,1,0:T(8,128)(2,1)S(1)}, bf16[2,4,128,128]{3,2,1,0:T(8,128)(2,1)S(1)}, u32[]{:S(2)}, u32[]{:S(2)}) collective-permute-start(bf16[2,4,128,128]{3,2,1,0:T(8,128)(2,1)S(1)} %collective-permute-done.refs_0_), channel_id=1, source_target_pairs={{0,129},{2,131},{4,133},{6,135},{8,137},{10,139},{12,141},{14,143}... | collective-permute-start | bytes 786440 | tf_op jit(solution)/shard_map/ppermute | solution.py:37
  16.9 1.3 %collective-permute-start.4 = (bf16[2,4,128,128]{3,2,1,0:T(8,128)(2,1)S(1)}, bf16[2,4,128,128]{3,2,1,0:T(8,128)(2,1)S(1)}, u32[]{:S(2)}, u32[]{:S(2)}) collective-permute-start(bf16[2,4,128,128]{3,2,1,0:T(8,128)(2,1)S(1)} %get-tuple-element.43), channel_id=1, source_target_pairs={{0,129},{2,131},{4,133},{6,135},{8,137},{10,139},{12,141},{14,143}... | collective-permute-start | bytes 786440 | tf_op jit(solution)/shard_map/ppermute | solution.py:37
  18.2 0.0 collective-permute-done.1.refs_1_
  18.3 1.3 %collective-permute-start.5 = (bf16[2,4,128,128]{3,2,1,0:T(8,128)(2,1)S(1)}, bf16[2,4,128,128]{3,2,1,0:T(8,128)(2,1)S(1)}, u32[]{:S(2)}, u32[]{:S(2)}) collective-permute-start(bf16[2,4,128,128]{3,2,1,0:T(8,128)(2,1)S(1)} %get-tuple-element.46), channel_id=1, source_target_pairs={{128,0},{130,2},{132,4},{134,6},{136,8},{138,10},{140,12},{142,14}... | collective-permute-start | bytes 786440 | tf_op jit(solution)/shard_map/ppermute | solution.py:37
  19.6 1.3 %collective-permute-start.6 = (bf16[2,4,128,128]{3,2,1,0:T(8,128)(2,1)S(1)}, bf16[2,4,128,128]{3,2,1,0:T(8,128)(2,1)S(1)}, u32[]{:S(2)}, u32[]{:S(2)}) collective-permute-start(bf16[2,4,128,128]{3,2,1,0:T(8,128)(2,1)S(1)} %get-tuple-element.47), channel_id=1, source_target_pairs={{129,0},{131,2},{133,4},{135,6},{137,8},{139,10},{141,12},{143,14}... | collective-permute-start | bytes 786440 | tf_op jit(solution)/shard_map/ppermute | solution.py:37
  20.9 0.0 collective-permute-done.3.refs_2_.refs_1_
  20.9 1.7 %collective-permute-done.2.refs_1_ = bf16[2,4,128,128]{3,2,1,0:T(8,128)(2,1)S(1)} collective-permute-done((bf16[2,4,128,128]{3,2,1,0:T(8,128)(2,1)S(1)}, bf16[2,4,128,128]{3,2,1,0:T(8,128)(2,1)S(1)}, u32[]{:S(2)}, u32[]{:S(2)}) %collective-permute-start.2) | collective-permute-done | bytes 262176 | tf_op jit(solution)/shard_map/ppermute | solution.py:37
  22.6 1.3 %collective-permute-start.7 = (bf16[2,4,128,128]{3,2,1,0:T(8,128)(2,1)S(1)}, bf16[2,4,128,128]{3,2,1,0:T(8,128)(2,1)S(1)}, u32[]{:S(2)}, u32[]{:S(2)}) collective-permute-start(bf16[2,4,128,128]{3,2,1,0:T(8,128)(2,1)S(1)} %get-tuple-element.48), channel_id=1, source_target_pairs={{1,0},{3,2},{5,4},{7,6},{9,8},{11,10},{13,12},{15,14},{17,16},{19,... | collective-permute-start | bytes 786440 | tf_op jit(solution)/shard_map/ppermute | solution.py:37
  23.9 7.3 %collective-permute-start.8 = (bf16[2,4,128,128]{3,2,1,0:T(8,128)(2,1)S(1)}, bf16[2,4,128,128]{3,2,1,0:T(8,128)(2,1)S(1)}, u32[]{:S(2)}, u32[]{:S(2)}) collective-permute-start(bf16[2,4,128,128]{3,2,1,0:T(8,128)(2,1)S(1)} %get-tuple-element.49), channel_id=1, source_target_pairs={{0,129},{2,131},{4,133},{6,135},{8,137},{10,139},{12,141},{14,143}... | collective-permute-start | bytes 786440 | tf_op jit(solution)/shard_map/ppermute | solution.py:37
  31.2 0.0 collective-permute-done.4.refs_2_
  31.3 1.3 %collective-permute-start.9 = (bf16[2,4,128,128]{3,2,1,0:T(8,128)(2,1)S(1)}, bf16[2,4,128,128]{3,2,1,0:T(8,128)(2,1)S(1)}, u32[]{:S(2)}, u32[]{:S(2)}) collective-permute-start(bf16[2,4,128,128]{3,2,1,0:T(8,128)(2,1)S(1)} %get-tuple-element.54), channel_id=1, source_target_pairs={{128,0},{130,2},{132,4},{134,6},{136,8},{138,10},{140,12},{142,14}... | collective-permute-start | bytes 786440 | tf_op jit(solution)/shard_map/ppermute | solution.py:37
  32.6 0.0 collective-permute-done.5.refs_1_
  32.6 1.3 %collective-permute-start.10 = (bf16[2,4,128,128]{3,2,1,0:T(8,128)(2,1)S(1)}, bf16[2,4,128,128]{3,2,1,0:T(8,128)(2,1)S(1)}, u32[]{:S(2)}, u32[]{:S(2)}) collective-permute-start(bf16[2,4,128,128]{3,2,1,0:T(8,128)(2,1)S(1)} %get-tuple-element.55), channel_id=1, source_target_pairs={{129,0},{131,2},{133,4},{135,6},{137,8},{139,10},{141,12},{143,14}... | collective-permute-start | bytes 786440 | tf_op jit(solution)/shard_map/ppermute | solution.py:37
  33.9 0.2 collective-permute-done.6.refs_2_
  34.0 0.0 collective-permute-done.7.refs_3_
  34.0 1.0 %collective-permute-done.8.refs_4_ = bf16[2,4,128,128]{3,2,1,0:T(8,128)(2,1)S(1)} collective-permute-done((bf16[2,4,128,128]{3,2,1,0:T(8,128)(2,1)S(1)}, bf16[2,4,128,128]{3,2,1,0:T(8,128)(2,1)S(1)}, u32[]{:S(2)}, u32[]{:S(2)}) %collective-permute-start.8) | collective-permute-done | bytes 262176 | tf_op jit(solution)/shard_map/ppermute | solution.py:37
  35.1 0.1 near1.1
  35.2 1.5 %collective-permute-start.11 = (bf16[2,4,128,128]{3,2,1,0:T(8,128)(2,1)S(1)}, bf16[2,4,128,128]{3,2,1,0:T(8,128)(2,1)S(1)}, u32[]{:S(2)}, u32[]{:S(2)}) collective-permute-start(bf16[2,4,128,128]{3,2,1,0:T(8,128)(2,1)S(1)} %get-tuple-element.56), channel_id=1, source_target_pairs={{1,0},{3,2},{5,4},{7,6},{9,8},{11,10},{13,12},{15,14},{17,16},{19,... | collective-permute-start | bytes 786440 | tf_op jit(solution)/shard_map/ppermute | solution.py:37
  36.6 4.3 %diag.1 = (bf16[64,128,128]{2,1,0:T(8,128)(2,1)}, bf16[8,128,128]{2,1,0:T(8,128)(2,1)}, bf16[8,128,128]{2,1,0:T(8,128)(2,1)}, f32[2,4,128,128]{3,2,1,0:T(8,128)S(1)}) custom-call(bf16[64,128,128]{2,1,0:T(8,128)(2,1)S(1)} %get-tuple-element.37.q_ref, bf16[64,128,128]{2,1,0:T(8,128)(2,1)S(1)} %get-tuple-element.38.g_ref, ...), custom_call_target="tpu_custom_call" | custom-call | flops 1 | bytes 1048576 | tf_op jit(solution)/shard_map/diag/pallas_call | solution.py:280
  40.9 0.0 collective-permute-done.9.rx_ref
  40.9 5.0 %collective-permute-done.10.ry_ref = bf16[2,4,128,128]{3,2,1,0:T(8,128)(2,1)S(1)} collective-permute-done((bf16[2,4,128,128]{3,2,1,0:T(8,128)(2,1)S(1)}, bf16[2,4,128,128]{3,2,1,0:T(8,128)(2,1)S(1)}, u32[]{:S(2)}, u32[]{:S(2)}) %collective-permute-start.10) | collective-permute-done | bytes 262176 | tf_op jit(solution)/shard_map/ppermute | solution.py:37
  45.9 0.0 collective-permute-done.11.rz_ref
  45.9 0.8 %final.1 = (bf16[8,128,128]{2,1,0:T(8,128)(2,1)}, bf16[8,128,128]{2,1,0:T(8,128)(2,1)}) custom-call(f32[2,4,128,128]{3,2,1,0:T(8,128)S(1)} %get-tuple-element.53.dkv_ref, bf16[2,4,128,128]{3,2,1,0:T(8,128)(2,1)S(1)} %collective-permute-done.9.rx_ref, ...), custom_call_target="tpu_custom_call", output_to_operand_aliasing={{0}: (4, {}), {1}: (5, {})} | custom-call | flops 1 | bytes 1048576 | tf_op jit(solution)/shard_map/final/pallas_call | solution.py:293
  (3 shorter events, 0.1 us)
Async XLA Ops:
  3.2 8.6 %collective-permute-start = (bf16[2,4,128,128]{3,2,1,0:T(8,128)(2,1)S(1)}, bf16[2,4,128,128]{3,2,1,0:T(8,128)(2,1)S(1)}, u32[]{:S(2)}, u32[]{:S(2)}) collective-permute-start(bf16[2,4,128,128]{3,2,1,0:T(8,128)(2,1)S(1)} %get-tuple-element.41.refs_0_), channel_id=1, source_target_pairs={{0,128},{2,130},{4,132},{6,134},{8,136},{10,138},{12,140},{14,142}... | collective-permute-start | bytes 786440 | tf_op jit(solution)/shard_map/ppermute | solution.py:37
  6.6 11.7 %collective-permute-start.1 = (bf16[2,4,128,128]{3,2,1,0:T(8,128)(2,1)S(1)}, bf16[2,4,128,128]{3,2,1,0:T(8,128)(2,1)S(1)}, u32[]{:S(2)}, u32[]{:S(2)}) collective-permute-start(bf16[2,4,128,128]{3,2,1,0:T(8,128)(2,1)S(1)} %get-tuple-element.41.refs_0_), channel_id=1, source_target_pairs={{0,129},{2,131},{4,133},{6,135},{8,137},{10,139},{12,141},{14,143}... | collective-permute-start | bytes 786440 | tf_op jit(solution)/shard_map/ppermute | solution.py:37
  9.3 11.6 %collective-permute-start.3 = (bf16[2,4,128,128]{3,2,1,0:T(8,128)(2,1)S(1)}, bf16[2,4,128,128]{3,2,1,0:T(8,128)(2,1)S(1)}, u32[]{:S(2)}, u32[]{:S(2)}) collective-permute-start(bf16[2,4,128,128]{3,2,1,0:T(8,128)(2,1)S(1)} %get-tuple-element.43), channel_id=1, source_target_pairs={{0,128},{2,130},{4,132},{6,134},{8,136},{10,138},{12,140},{14,142}... | collective-permute-start | bytes 786440 | tf_op jit(solution)/shard_map/ppermute | solution.py:37
  11.8 10.8 %collective-permute-start.2 = (bf16[2,4,128,128]{3,2,1,0:T(8,128)(2,1)S(1)}, bf16[2,4,128,128]{3,2,1,0:T(8,128)(2,1)S(1)}, u32[]{:S(2)}, u32[]{:S(2)}) collective-permute-start(bf16[2,4,128,128]{3,2,1,0:T(8,128)(2,1)S(1)} %collective-permute-done.refs_0_), channel_id=1, source_target_pairs={{0,129},{2,131},{4,133},{6,135},{8,137},{10,139},{12,141},{14,143}... | collective-permute-start | bytes 786440 | tf_op jit(solution)/shard_map/ppermute | solution.py:37
  16.9 14.3 %collective-permute-start.4 = (bf16[2,4,128,128]{3,2,1,0:T(8,128)(2,1)S(1)}, bf16[2,4,128,128]{3,2,1,0:T(8,128)(2,1)S(1)}, u32[]{:S(2)}, u32[]{:S(2)}) collective-permute-start(bf16[2,4,128,128]{3,2,1,0:T(8,128)(2,1)S(1)} %get-tuple-element.43), channel_id=1, source_target_pairs={{0,129},{2,131},{4,133},{6,135},{8,137},{10,139},{12,141},{14,143}... | collective-permute-start | bytes 786440 | tf_op jit(solution)/shard_map/ppermute | solution.py:37
  18.3 14.3 %collective-permute-start.5 = (bf16[2,4,128,128]{3,2,1,0:T(8,128)(2,1)S(1)}, bf16[2,4,128,128]{3,2,1,0:T(8,128)(2,1)S(1)}, u32[]{:S(2)}, u32[]{:S(2)}) collective-permute-start(bf16[2,4,128,128]{3,2,1,0:T(8,128)(2,1)S(1)} %get-tuple-element.46), channel_id=1, source_target_pairs={{128,0},{130,2},{132,4},{134,6},{136,8},{138,10},{140,12},{142,14}... | collective-permute-start | bytes 786440 | tf_op jit(solution)/shard_map/ppermute | solution.py:37
  19.6 14.5 %collective-permute-start.6 = (bf16[2,4,128,128]{3,2,1,0:T(8,128)(2,1)S(1)}, bf16[2,4,128,128]{3,2,1,0:T(8,128)(2,1)S(1)}, u32[]{:S(2)}, u32[]{:S(2)}) collective-permute-start(bf16[2,4,128,128]{3,2,1,0:T(8,128)(2,1)S(1)} %get-tuple-element.47), channel_id=1, source_target_pairs={{129,0},{131,2},{133,4},{135,6},{137,8},{139,10},{141,12},{143,14}... | collective-permute-start | bytes 786440 | tf_op jit(solution)/shard_map/ppermute | solution.py:37
  22.6 11.4 %collective-permute-start.7 = (bf16[2,4,128,128]{3,2,1,0:T(8,128)(2,1)S(1)}, bf16[2,4,128,128]{3,2,1,0:T(8,128)(2,1)S(1)}, u32[]{:S(2)}, u32[]{:S(2)}) collective-permute-start(bf16[2,4,128,128]{3,2,1,0:T(8,128)(2,1)S(1)} %get-tuple-element.48), channel_id=1, source_target_pairs={{1,0},{3,2},{5,4},{7,6},{9,8},{11,10},{13,12},{15,14},{17,16},{19,... | collective-permute-start | bytes 786440 | tf_op jit(solution)/shard_map/ppermute | solution.py:37
  23.9 11.2 %collective-permute-start.8 = (bf16[2,4,128,128]{3,2,1,0:T(8,128)(2,1)S(1)}, bf16[2,4,128,128]{3,2,1,0:T(8,128)(2,1)S(1)}, u32[]{:S(2)}, u32[]{:S(2)}) collective-permute-start(bf16[2,4,128,128]{3,2,1,0:T(8,128)(2,1)S(1)} %get-tuple-element.49), channel_id=1, source_target_pairs={{0,129},{2,131},{4,133},{6,135},{8,137},{10,139},{12,141},{14,143}... | collective-permute-start | bytes 786440 | tf_op jit(solution)/shard_map/ppermute | solution.py:37
  31.3 9.7 %collective-permute-start.9 = (bf16[2,4,128,128]{3,2,1,0:T(8,128)(2,1)S(1)}, bf16[2,4,128,128]{3,2,1,0:T(8,128)(2,1)S(1)}, u32[]{:S(2)}, u32[]{:S(2)}) collective-permute-start(bf16[2,4,128,128]{3,2,1,0:T(8,128)(2,1)S(1)} %get-tuple-element.54), channel_id=1, source_target_pairs={{128,0},{130,2},{132,4},{134,6},{136,8},{138,10},{140,12},{142,14}... | collective-permute-start | bytes 786440 | tf_op jit(solution)/shard_map/ppermute | solution.py:37
  32.6 13.4 %collective-permute-start.10 = (bf16[2,4,128,128]{3,2,1,0:T(8,128)(2,1)S(1)}, bf16[2,4,128,128]{3,2,1,0:T(8,128)(2,1)S(1)}, u32[]{:S(2)}, u32[]{:S(2)}) collective-permute-start(bf16[2,4,128,128]{3,2,1,0:T(8,128)(2,1)S(1)} %get-tuple-element.55), channel_id=1, source_target_pairs={{129,0},{131,2},{133,4},{135,6},{137,8},{139,10},{141,12},{143,14}... | collective-permute-start | bytes 786440 | tf_op jit(solution)/shard_map/ppermute | solution.py:37
  35.2 10.8 %collective-permute-start.11 = (bf16[2,4,128,128]{3,2,1,0:T(8,128)(2,1)S(1)}, bf16[2,4,128,128]{3,2,1,0:T(8,128)(2,1)S(1)}, u32[]{:S(2)}, u32[]{:S(2)}) collective-permute-start(bf16[2,4,128,128]{3,2,1,0:T(8,128)(2,1)S(1)} %get-tuple-element.56), channel_id=1, source_target_pairs={{1,0},{3,2},{5,4},{7,6},{9,8},{11,10},{13,12},{15,14},{17,16},{19,... | collective-permute-start | bytes 786440 | tf_op jit(solution)/shard_map/ppermute | solution.py:37
